TPU v7x, 128 devices: a whole 4x4x4 slice. The times are simulated.
128 devices in a mesh: gx: 8 (over z, y_hi), gy: 4 (over x), gz: 4 (over y_lo, core).
Axes of the slice: x: 4, y: 4 (y_hi: 2, y_lo: 2; y = y_hi * 2 + y_lo), z: 4, core: 2. Of those that a mesh axis runs over, the one named last changes fastest.
Arguments:
- normed: bfloat16 [2560, 6144], P(('gx', 'gy'), 'gz'), may hold values from -6 to 6
- context: bfloat16 [2560, 6144], P('gz', ('gx', 'gy')), may hold values from -6 to 6
- hidden_pre: bfloat16 [2560, 24576], P('gz', ('gx', 'gy')), may hold values from -6 to 6
- grad_out: bfloat16 [2560, 6144], P(('gx', 'gy'), 'gz'), may hold values from -6 to 6
- w_in: bfloat16 [6144, 24576], P('gz', ('gx', 'gy')), may hold values from -0.078125 to 0.078125
- w_out: bfloat16 [24576, 6144], P(('gx', 'gy'), 'gz'), may hold values from -0.0390625 to 0.0390625
- w_proj: bfloat16 [6144, 6144], P(('gx', 'gy'), 'gz'), may hold values from -0.078125 to 0.078125
Outputs:
- grad_normed: bfloat16 [2560, 6144], P(('gx', 'gy'), 'gz')
- grad_context: bfloat16 [2560, 6144], P('gz', ('gx', 'gy'))
- grad_w_in: bfloat16 [6144, 24576], P('gz', ('gx', 'gy'))
- grad_w_out: bfloat16 [24576, 6144], P(('gx', 'gy'), 'gz')
- grad_w_proj: bfloat16 [6144, 6144], P(('gx', 'gy'), 'gz')
All inputs are finite; a program needn't handle non-finite values.
Results may differ from a plain program's by a relative error of at most 0.0051.
Values may be sent and summed in bfloat16 or wider, within the bound.
A program may use at most 128 MiB of HBM per device.

v0:
```python
import math

import jax
import jax.numpy as jnp
from jax import lax
from jax.sharding import PartitionSpec as P

inv_root_two = 0.7071067811865476
inv_root_two_pi = 0.3989422804014327


def gelu_parts(hidden_pre):
    values = hidden_pre.astype(jnp.float32)
    normal_cdf = 0.5 * (1.0 + jax.scipy.special.erf(values * inv_root_two))
    density = jnp.exp(-0.5 * values * values) * inv_root_two_pi
    return (values * normal_cdf, normal_cdf + values * density)


def contract_rows(left, right):
    return lax.dot_general(
        left, right, (((0,), (0,)), ((), ())), preferred_element_type=jnp.float32
    )


def contract_cols(left, right):
    return lax.dot_general(
        left, right, (((1,), (1,)), ((), ())), preferred_element_type=jnp.float32
    )


def body(normed, context, hidden_pre, grad_out, w_in, w_out, w_proj):
    grad_full, normed_full = (
        lax.all_gather(grad_out, ("gx", "gy"), axis=0, tiled=True),
        lax.all_gather(normed, ("gx", "gy"), axis=0, tiled=True),
    )
    hidden_full, context_full = (
        lax.all_gather(hidden_pre, "gz", axis=0, tiled=True),
        lax.all_gather(context, "gz", axis=0, tiled=True),
    )
    grad_scale = 1.0 / math.sqrt(grad_full.shape[0])
    activated_f, slope_full = gelu_parts(hidden_full)
    activated = activated_f.astype(jnp.bfloat16)
    panel = grad_full
    grad_share = lax.psum_scatter(
        contract_cols(panel, w_out), "gz", scatter_dimension=0, tiled=True
    )
    local_act, local_slope = gelu_parts(hidden_pre)
    hidden_share = (grad_share * local_slope).astype(jnp.bfloat16)
    grad_hidden = lax.all_gather(hidden_share, "gz", axis=0, tiled=True)
    grad_w_out = (contract_rows(activated, grad_full) * grad_scale).astype(jnp.bfloat16)
    grad_w_in = (contract_rows(normed_full, grad_hidden) * grad_scale).astype(jnp.bfloat16)
    grad_w_proj = (contract_rows(context_full, grad_full) * grad_scale).astype(jnp.bfloat16)
    panel = grad_hidden
    grad_normed = lax.psum_scatter(
        contract_cols(panel, w_in), ("gx", "gy"), scatter_dimension=0, tiled=True
    ).astype(jnp.bfloat16)
    panel = grad_full
    grad_context = lax.psum_scatter(
        contract_cols(panel, w_proj), "gz", scatter_dimension=0, tiled=True
    ).astype(jnp.bfloat16)
    return (grad_normed, grad_context, grad_w_in, grad_w_out, grad_w_proj)


def solution(mesh):
    in_specs = (
        P(("gx", "gy"), "gz"),
        P("gz", ("gx", "gy")),
        P("gz", ("gx", "gy")),
        P(("gx", "gy"), "gz"),
        P("gz", ("gx", "gy")),
        P(("gx", "gy"), "gz"),
        P(("gx", "gy"), "gz"),
    )
    out_specs = (
        P(("gx", "gy"), "gz"),
        P("gz", ("gx", "gy")),
        P("gz", ("gx", "gy")),
        P(("gx", "gy"), "gz"),
        P(("gx", "gy"), "gz"),
    )
    return jax.shard_map(body, mesh=mesh, in_specs=in_specs, out_specs=out_specs, check_vma=False)
```

profile of v0, /device:TPU:0, one launch (start us, length us, event | category | flops | bytes accessed | tf_op | source)
XLA Modules:
  0.0 712.2 jit_solution(3424751733002135623)
XLA Ops:
  7.2 0.0 all-gather.5.cloned.1.call-start
  7.2 0.7 all-gather.5.cloned.1.call-update
  7.9 0.0 reduce-scatter.4.cloned.1.call-start
  8.0 106.9 %all-gather.5.cloned.1.call-done = bf16[2560,1536]{1,0:T(8,128)(2,1)} async-done(((bf16[80,1536]{1,0:T(8,128)(2,1)}), bf16[2560,1536]{1,0:T(8,128)(2,1)}) %all-gather.5.cloned.1.call-update) | async-done | bytes 7864336 | tf_op jit(solution)/shard_map/all_gather | solution.py:33
  114.8 11.2 %fusion.21 = f32[2560,768]{1,0:T(8,128)} fusion(bf16[2560,1536]{1,0:T(8,128)(2,1)} %all-gather.5.cloned.1.call-done, bf16[768,1536]{1,0:T(8,128)(2,1)} %param.12), kind=kOutput, calls=%fused_computation.29 | convolution fusion | flops 6039797760 | bytes 18087936 | tf_op jit(solution)/shard_map/dot_general | solution.py:26
  126.1 0.0 reduce-scatter.4.cloned.1.call-update
  126.1 0.0 all-gather.7.cloned.1.call-start
  126.2 73.2 %reduce-scatter.4.cloned.1.call-done = f32[640,768]{1,0:T(8,128)} async-done(((f32[2560,768]{1,0:T(8,128)}), f32[640,768]{1,0:T(8,128)}) %reduce-scatter.4.cloned.1.call-update) | async-done | bytes 1966096 | tf_op jit(solution)/shard_map/reduce_scatter | solution.py:44
  199.3 3.3 fusion.17
  202.7 0.0 all-gather.7.cloned.1.call-update
  202.7 0.0 all-gather.11.cloned.1.call-start
  202.7 0.5 all-gather.11.cloned.1.call-update
  203.3 0.0 reduce-scatter.8.cloned.1.call-start
  203.3 7.3 %fusion.23 = f32[2560,192]{0,1:T(8,128)} fusion(bf16[2560,1536]{1,0:T(8,128)(2,1)} %all-gather.5.cloned.1.call-done, bf16[192,1536]{1,0:T(8,128)(2,1)} %param.13), kind=kOutput, calls=%fused_computation.31 | convolution fusion | flops 1509949440 | bytes 10420224 | tf_op jit(solution)/shard_map/dot_general | solution.py:26
  210.6 0.0 reduce-scatter.8.cloned.1.call-update
  210.6 0.0 all-gather.9.cloned.1.call-start
  210.7 0.5 all-gather.9.cloned.1.call-update
  211.2 0.0 reduce-scatter.6.cloned.1.call-start
  211.2 36.5 %all-gather.7.cloned.1.call-done = bf16[2560,768]{1,0:T(8,128)(2,1)} async-done(((bf16[640,768]{1,0:T(8,128)(2,1)}), bf16[2560,768]{1,0:T(8,128)(2,1)}) %all-gather.7.cloned.1.call-update) | async-done | bytes 3932176 | tf_op jit(solution)/shard_map/all_gather | solution.py:49
  247.7 11.4 %fusion.22 = f32[2560,1536]{1,0:T(8,128)} fusion(bf16[2560,768]{1,0:T(8,128)(2,1)} %all-gather.7.cloned.1.call-done, bf16[1536,768]{1,0:T(8,128)(2,1)S(1)} %copy-done), kind=kOutput, calls=%fused_computation.30 | convolution fusion | flops 6039797760 | bytes 22020096 | tf_op jit(solution)/shard_map/dot_general | solution.py:26
  259.1 1.0 copy-done.3
  260.1 15.5 %all_gather.19 = bf16[2560,192]{0,1:T(8,128)(2,1)S(1)} all-gather(bf16[640,192]{0,1:T(8,128)(2,1)S(1)} %copy-done.3), channel_id=1, replica_groups=mesh['gx'=8,'gy'=4,'gz'=4] {'gz'}, dimensions={0}, use_global_device_ids=true | all-gather | bytes 1228800 | tf_op jit(solution)/shard_map/all_gather | solution.py:38
  275.6 5.8 fusion.9
  281.5 18.4 %all-gather.11.cloned.1.call-done = bf16[2560,768]{1,0:T(8,128)(2,1)} async-done(((bf16[640,768]{1,0:T(8,128)(2,1)}), bf16[2560,768]{1,0:T(8,128)(2,1)}) %all-gather.11.cloned.1.call-update) | async-done | bytes 3932176 | tf_op jit(solution)/shard_map/all_gather | solution.py:37
  299.9 11.4 %multiply_convert_fusion = bf16[768,1536]{1,0:T(8,128)(2,1)} fusion(bf16[2560,1536]{1,0:T(8,128)(2,1)} %all-gather.5.cloned.1.call-done, bf16[2560,768]{1,0:T(8,128)(2,1)} %all-gather.11.cloned.1.call-done), kind=kOutput, calls=%fused_computation.6 | convolution fusion | flops 6053953536 | bytes 14155776 | tf_op jit(solution)/shard_map/dot_general | solution.py:20
  311.3 19.8 %reduce-scatter.8.cloned.1.call-done = f32[640,192]{0,1:T(8,128)} async-done(((f32[2560,192]{0,1:T(8,128)}), f32[640,192]{0,1:T(8,128)}) %reduce-scatter.8.cloned.1.call-update) | async-done | bytes 491536 | tf_op jit(solution)/shard_map/reduce_scatter | solution.py:58
  331.1 1.8 convert_element_type.33
  332.9 103.4 %all-gather.9.cloned.1.call-done = bf16[2560,1536]{1,0:T(8,128)(2,1)} async-done(((bf16[80,1536]{1,0:T(8,128)(2,1)}), bf16[2560,1536]{1,0:T(8,128)(2,1)}) %all-gather.9.cloned.1.call-update) | async-done | bytes 7864336 | tf_op jit(solution)/shard_map/all_gather | solution.py:34
  436.3 11.1 %fusion.8 = bf16[1536,768]{0,1:T(8,128)(2,1)} fusion(bf16[2560,768]{1,0:T(8,128)(2,1)} %all-gather.7.cloned.1.call-done, bf16[2560,1536]{1,0:T(8,128)(2,1)} %all-gather.9.cloned.1.call-done), kind=kOutput, calls=%fused_computation.15 | convolution fusion | flops 6042157056 | bytes 14155776 | tf_op jit(solution)/shard_map/dot_general | solution.py:20
  447.4 4.3 copy.12
  451.7 251.9 %reduce-scatter.6.cloned.1.call-done = f32[80,1536]{1,0:T(8,128)} async-done(((f32[2560,1536]{1,0:T(8,128)}), f32[80,1536]{1,0:T(8,128)}) %reduce-scatter.6.cloned.1.call-update) | async-done | bytes 491536 | tf_op jit(solution)/shard_map/reduce_scatter | solution.py:54
  703.6 1.7 convert_element_type.32
  (8 shorter events, 0.0 us)
Async XLA Ops:
  7.2 240.5 %copy-start = (bf16[1536,768]{1,0:T(8,128)(2,1)S(1)}, bf16[1536,768]{1,0:T(8,128)(2,1)}, u32[]{:S(2)}) copy-start(bf16[1536,768]{1,0:T(8,128)(2,1)} %param.11) | copy-start | bytes 7077892
  7.2 107.7 %all-gather.5.cloned.1.call-start = ((), (), s32[]{:S(2)}) async-start(), calls=%async_computation.3 | async-start | bytes 8110080 | tf_op jit(solution)/shard_map/all_gather | solution.py:33
  7.9 191.4 %reduce-scatter.4.cloned.1.call-start = ((), (), s32[]{:S(2)}) async-start(), calls=%async_computation.4 | async-start | bytes 9830400 | tf_op jit(solution)/shard_map/reduce_scatter | solution.py:44
  126.1 73.2 %copy-start.2 = (bf16[640,768]{1,0:T(8,128)(2,1)S(1)}, bf16[640,768]{1,0:T(8,128)(2,1)}, u32[]{:S(2)}) copy-start(bf16[640,768]{1,0:T(8,128)(2,1)} %param.9) | copy-start | bytes 2949124
  126.1 121.6 %all-gather.7.cloned.1.call-start = ((), (), s32[]{:S(2)}) async-start(), calls=%async_computation.5 | async-start | bytes 4915200 | tf_op jit(solution)/shard_map/all_gather | solution.py:49
  202.7 97.2 %all-gather.11.cloned.1.call-start = ((), (), s32[]{:S(2)}) async-start(), calls=%async_computation.9 | async-start | bytes 4915200 | tf_op jit(solution)/shard_map/all_gather | solution.py:37
  203.3 127.8 %reduce-scatter.8.cloned.1.call-start = ((), (), s32[]{:S(2)}) async-start(), calls=%async_computation.7 | async-start | bytes 2457600 | tf_op jit(solution)/shard_map/reduce_scatter | solution.py:58
  210.6 225.7 %all-gather.9.cloned.1.call-start = ((), (), s32[]{:S(2)}) async-start(), calls=%async_computation.8 | async-start | bytes 8110080 | tf_op jit(solution)/shard_map/all_gather | solution.py:34
  211.2 492.4 %reduce-scatter.6.cloned.1.call-start = ((), (), s32[]{:S(2)}) async-start(), calls=%async_computation.6 | async-start | bytes 16220160 | tf_op jit(solution)/shard_map/reduce_scatter | solution.py:54
  259.1 1.0 copy-start.3
  436.3 269.0 %copy-start.1 = (bf16[1536,768]{1,0:T(8,128)(2,1)S(1)}, bf16[1536,768]{1,0:T(8,128)(2,1)}, u32[]{:S(2)}) copy-start(bf16[1536,768]{1,0:T(8,128)(2,1)} %param.11) | copy-start | bytes 7077892
Sparse Core Ops, SparseCore 0:
  11.1 103.7 all-gather.4
  126.2 73.0 reduce-scatter.3
  202.8 44.8 all-gather.6
  249.2 50.6 all-gather.10
  302.7 28.3 reduce-scatter.7
  334.0 102.2 all-gather.8
  441.8 261.7 reduce-scatter.5
where the time goes:
time: 713 us; the launch traced here: 712 us
  waiting for transfers between devices  612 us (86%)
  matrix products  58.3 us (8%)
  blocking collectives  15.5 us (2%)
  between operations  14.1 us (2%)
    reduce_scatter x1, waiting for transfers between devices, body(): lax.psum_scatter(contract_cols(panel, w_in), ('gx', 'gy'), scatter_dimens...  252 us
    all_gather x1, waiting for transfers between devices, body(): lax.all_gather(grad_out, ('gx', 'gy'), axis=0, tiled=True)  107 us
    all_gather x1, waiting for transfers between devices, body(): lax.all_gather(normed, ('gx', 'gy'), axis=0, tiled=True)  103 us
    reduce_scatter x1, waiting for transfers between devices, body(): lax.psum_scatter(contract_cols(panel, w_out), 'gz', scatter_dimension=0,...  73.2 us
    all_gather x1, waiting for transfers between devices, body(): grad_hidden = lax.all_gather(hidden_share, 'gz', axis=0, tiled=True)  36.5 us
    dot_general x3, matrix products, contract_cols(): lax.dot_general(left, right, (((1,), (1,)), ((), ())), preferred_element_...  29.9 us
    dot_general x3, matrix products, contract_rows(): lax.dot_general(left, right, (((0,), (0,)), ((), ())), preferred_element_...  28.4 us
    reduce_scatter x1, waiting for transfers between devices, body(): lax.psum_scatter(contract_cols(panel, w_proj), 'gz', scatter_dimension=0,...  19.8 us
  transfers between devices with their start and end apart: 7, of which 7 were waited for; matrix products, arithmetic and copies ran while one was open for 7% of the time, Pallas kernels for 0%

commit v1 on v0

--- a/solution.py
+++ b/solution.py
@@ -3,8 +3,11 @@
 import jax
 import jax.numpy as jnp
 from jax import lax
+from jax.experimental import pallas as pl
+from jax.experimental.pallas import tpu as pltpu
 from jax.sharding import PartitionSpec as P
 
+MESH = pl.DeviceIdType.MESH
 inv_root_two = 0.7071067811865476
 inv_root_two_pi = 0.3989422804014327
 
@@ -28,11 +31,194 @@
     )
 
 
+class Place:
+    def __init__(self):
+        gx, gy, gz = (lax.axis_index(a) for a in ("gx", "gy", "gz"))
+        self.z, self.yh, self.x = gx // 2, lax.rem(gx, 2), gy
+        z, yh, x = self.z, self.yh, self.x
+        zp, zm, z2 = (lax.rem(z + k, 4) for k in (1, 3, 2))
+        xp, xm, x2 = (lax.rem(x + k, 4) for k in (1, 3, 2))
+        self.zs = (z, zp, zm, z2)
+        self.xs = (x, xp, xm, x2)
+        self.dev = {
+            "x+": (gx, xp, gz),
+            "x-": (gx, xm, gz),
+            "z+": (zp * 2 + yh, x, gz),
+            "z-": (zm * 2 + yh, x, gz),
+            "yh": (z * 2 + 1 - yh, x, gz),
+        }
+
+
+class Links:
+    def __init__(self, place, send_sems, recv_sems):
+        self.place, self.ss, self.rs = place, send_sems, recv_sems
+        self.names, self.started = {}, []
+
+    def copy(self, key, src, dst, to):
+        i = self.names.setdefault(key, len(self.names))
+        return pltpu.make_async_remote_copy(
+            src_ref=src, dst_ref=dst, send_sem=self.ss.at[i], recv_sem=self.rs.at[i],
+            device_id=self.place.dev[to], device_id_type=MESH)
+
+    def send(self, key, src, dst, to):
+        c = self.copy(key, src, dst, to)
+        c.start()
+        self.started.append(c)
+
+    def got(self, key, view):
+        self.copy(key, view, view, "x+").wait_recv()
+
+
+class Gather:
+    def __init__(self, name, full, place, links):
+        self.name, self.full, self.p, self.l = name, full, place, links
+        self.first = (("x+", "x-"), ("z+", "z-"))
+        self.second = (("z+", "z-"), ("x+", "x-"))
+        self.one = (place.xs, place.zs)
+        self.two = (place.zs, place.xs)
+
+    def view(self, part, yy, i, j, half=None):
+        zz, xx = (j, i) if part == 0 else (i, j)
+        width = self.full.shape[-1] // 2
+        start, n = part * width, width
+        if half is not None:
+            n = width // 2
+            start += half * n
+        return self.full.at[zz, yy, xx, :, pl.ds(start, n)]
+
+    def send(self, key, view, to):
+        self.l.send((self.name,) + key, view, view, to)
+
+    def got(self, key, view):
+        self.l.got((self.name,) + key, view)
+
+    def exchange(self):
+        own = self.full.at[self.p.z, self.p.yh, self.p.x]
+        self.send(("y",), own, "yh")
+
+    def exchanged(self):
+        self.got(("y",), self.full.at[self.p.z, self.p.yh, self.p.x])
+
+    def r0(self, w, yy):
+        for key, ways in (("f", self.first), ("s0", self.second)):
+            for p in (0, 1):
+                own = self.view(p, yy, self.one[p][0], self.two[p][0])
+                for s in (0, 1):
+                    self.send((w, p, key, s), own, ways[p][s])
+
+    def r1(self, w, yy):
+        for p in (0, 1):
+            i0, ip, im, i2 = self.one[p]
+            j0 = self.two[p][0]
+            self.got((w, p, "f", 0), self.view(p, yy, im, j0))
+            self.send((w, p, "ff", 0), self.view(p, yy, im, j0, 0), self.first[p][0])
+            self.got((w, p, "f", 1), self.view(p, yy, ip, j0))
+            self.send((w, p, "ff", 1), self.view(p, yy, ip, j0, 1), self.first[p][1])
+        for p in (0, 1):
+            i0, ip, im, i2 = self.one[p]
+            j0 = self.two[p][0]
+            for k, i in (("s1", im), ("s2", ip)):
+                for s in (0, 1):
+                    self.send((w, p, k, s), self.view(p, yy, i, j0), self.second[p][s])
+
+    def r2(self, w, yy):
+        for p in (0, 1):
+            i2, j0 = self.one[p][3], self.two[p][0]
+            for h in (0, 1):
+                self.got((w, p, "ff", h), self.view(p, yy, i2, j0, h))
+            for s in (0, 1):
+                self.send((w, p, "s3", s), self.view(p, yy, i2, j0), self.second[p][s])
+
+    def order(self, p, k):
+        i0, ip, im, i2 = self.one[p]
+        return (i0, im, ip, i2)[k]
+
+    def r3(self, w, yy, k):
+        for p in (0, 1):
+            i = self.order(p, k)
+            j0, jp, jm, j2 = self.two[p]
+            self.got((w, p, f"s{k}", 0), self.view(p, yy, i, jm))
+            self.send((w, p, f"sf{k}", 0), self.view(p, yy, i, jm, 0), self.second[p][0])
+            self.got((w, p, f"s{k}", 1), self.view(p, yy, i, jp))
+            self.send((w, p, f"sf{k}", 1), self.view(p, yy, i, jp, 1), self.second[p][1])
+
+    def r4(self, w, yy, k):
+        for p in (0, 1):
+            i, j2 = self.order(p, k), self.two[p][3]
+            for h in (0, 1):
+                self.got((w, p, f"sf{k}", h), self.view(p, yy, i, j2, h))
+
+
+SEMS = 192
+
+
+def gather_kernel(g_ref, n_ref, g_full, n_full, ss, rs, lsem):
+    place = Place()
+    z, yh, x = place.z, place.yh, place.x
+    bar = pltpu.get_barrier_semaphore()
+    for d in place.dev.values():
+        pl.semaphore_signal(bar, inc=1, device_id=d, device_id_type=MESH)
+    local = [
+        pltpu.make_async_copy(g_ref, g_full.at[z, yh, x], lsem.at[0]),
+        pltpu.make_async_copy(n_ref, n_full.at[z, yh, x], lsem.at[1]),
+    ]
+    for c in local:
+        c.start()
+    pl.semaphore_wait(bar, len(place.dev))
+    for c in local:
+        c.wait()
+    links = Links(place, ss, rs)
+    a, b = Gather("g", g_full, place, links), Gather("n", n_full, place, links)
+    o = 1 - yh
+    a.exchange()
+    b.exchange()
+    a.r0(0, yh)
+    a.r1(0, yh)
+    a.r3(0, yh, 0)
+    a.r2(0, yh)
+    a.exchanged()
+    waves = [(a, 0, yh), (a, 1, o), (b, 0, yh), (b, 1, o)]
+    for k, (u, w, yy) in enumerate(waves):
+        after = waves[k + 1] if k + 1 < len(waves) else None
+        if after:
+            v, w2, y2 = after
+            if k == 2:
+                b.exchanged()
+            v.r0(w2, y2)
+        u.r3(w, yy, 1)
+        u.r3(w, yy, 2)
+        if after:
+            v.r1(w2, y2)
+        u.r3(w, yy, 3)
+        if after:
+            v.r3(w2, y2, 0)
+            v.r2(w2, y2)
+        for j in range(4):
+            u.r4(w, yy, j)
+    for c in links.started:
+        c.wait_send()
+
+
+def gather_both(grad_out, normed):
+    shape = jax.ShapeDtypeStruct((4, 2, 4) + grad_out.shape, grad_out.dtype)
+    g, n = pl.pallas_call(
+        gather_kernel,
+        out_shape=[shape, shape],
+        in_specs=[pl.BlockSpec(memory_space=pl.ANY)] * 2,
+        out_specs=[pl.BlockSpec(memory_space=pl.ANY)] * 2,
+        scratch_shapes=[
+            pltpu.SemaphoreType.DMA((SEMS,)),
+            pltpu.SemaphoreType.DMA((SEMS,)),
+            pltpu.SemaphoreType.DMA((2,)),
+        ],
+        compiler_params=pltpu.CompilerParams(collective_id=0, has_side_effects=True),
+    )(grad_out, normed)
+    rows = 32 * grad_out.shape[0]
+    return g.reshape(rows, grad_out.shape[1]), n.reshape(rows, grad_out.shape[1])
+
+
 def body(normed, context, hidden_pre, grad_out, w_in, w_out, w_proj):
-    grad_full, normed_full = (
-        lax.all_gather(grad_out, ("gx", "gy"), axis=0, tiled=True),
-        lax.all_gather(normed, ("gx", "gy"), axis=0, tiled=True),
-    )
+    grad_full, normed_full = gather_both(grad_out, normed)
     hidden_full, context_full = (
         lax.all_gather(hidden_pre, "gz", axis=0, tiled=True),
         lax.all_gather(context, "gz", axis=0, tiled=True),

time: 713 us -> 610 us (0.86)
  waiting for transfers between devices: 612 us -> 409 us
  Pallas kernels: 0 us -> 106 us
    all_gather x2 -> x0, waiting for transfers between devices: 210 us -> none  [the longest x1 107 us: body(): lax.all_gather(grad_out, ('gx', 'gy'), axis=0, tiled=True)]
    pallas_call x0 -> x1, Pallas kernels: none -> 106 us  [gather_both(): pl.pallas_call(gather_kernel, out_shape=[shape, shape], in_specs=[pl.Bloc...]
    all_gather x1, waiting for transfers between devices: 18.4 us -> 44.6 us  [body(): lax.all_gather(hidden_pre, 'gz', axis=0, tiled=True)]
    reduce_scatter x1, waiting for transfers between devices: 19.8 us -> 3.04 us  [body(): lax.psum_scatter(contract_cols(panel, w_proj), 'gz', scatter_dimension=0,...]
  transfers between devices with their start and end apart: 7 -> 5, of which waited for: 7 -> 5; matrix products, arithmetic and copies ran while one was open for 7% -> 8% of each run, Pallas kernels for 0% -> 0%
where the time goes in v1:
time: 610 us
  waiting for transfers between devices  409 us (67%)
  Pallas kernels  106 us (17%)
  matrix products  57.1 us (9%)
  blocking collectives  15.6 us (3%)
  between operations  13.8 us (2%)
  other arithmetic  6.85 us (1%)
    reduce_scatter x1, waiting for transfers between devices, body(): lax.psum_scatter(contract_cols(panel, w_in), ('gx', 'gy'), scatter_dimens...  249 us
    pallas_call x1, Pallas kernels, gather_both(): pl.pallas_call(gather_kernel, out_shape=[shape, shape], in_specs=[pl.Bloc...  106 us
    reduce_scatter x1, waiting for transfers between devices, body(): lax.psum_scatter(contract_cols(panel, w_out), 'gz', scatter_dimension=0,...  74.7 us
    all_gather x1, waiting for transfers between devices, body(): lax.all_gather(hidden_pre, 'gz', axis=0, tiled=True)  44.6 us
    all_gather x1, waiting for transfers between devices, body(): grad_hidden = lax.all_gather(hidden_share, 'gz', axis=0, tiled=True)  37 us
    dot_general x3, matrix products, contract_cols(): lax.dot_general(left, right, (((1,), (1,)), ((), ())), preferred_element_...  29.9 us
    dot_general x3, matrix products, contract_rows(): lax.dot_general(left, right, (((0,), (0,)), ((), ())), preferred_element_...  27.2 us
    all_gather x1, blocking collectives, body(): lax.all_gather(context, 'gz', axis=0, tiled=True)  15.6 us
  transfers between devices with their start and end apart: 5, of which 5 were waited for; matrix products, arithmetic and copies ran while one was open for 8% of the time, Pallas kernels for 0%

profile of v1, /device:TPU:0, one launch (start us, length us, event | category | flops | bytes accessed | tf_op | source)
XLA Modules:
  0.0 610.1 jit_solution(2122470149528091975)
XLA Ops:
  7.2 0.0 copy-start
  7.2 0.0 reduce-scatter.4.cloned.1.call-start
  7.2 106.3 %shard_map.110 = (bf16[4,2,4,80,1536]{4,3,2,1,0:T(8,128)(2,1)}, bf16[4,2,4,80,1536]{4,3,2,1,0:T(8,128)(2,1)}) custom-call(bf16[80,1536]{1,0:T(8,128)(2,1)} %g_ref.1, bf16[80,1536]{1,0:T(8,128)(2,1)} %n_ref.1), custom_call_target="tpu_custom_call" | custom-call | tf_op jit(solution)/shard_map/pallas_call | solution.py:204
  113.5 11.3 %fusion.21 = f32[2560,768]{1,0:T(8,128)} fusion(bf16[2560,1536]{1,0:T(8,128)(2,1)} %bitcast.16, bf16[768,1536]{1,0:T(8,128)(2,1)} %param.12), kind=kOutput, calls=%fused_computation.29 | convolution fusion | flops 6039797760 | bytes 18087936 | tf_op jit(solution)/shard_map/dot_general | solution.py:29
  124.8 0.0 copy-start.1
  124.8 0.0 reduce-scatter.4.cloned.1.call-update
  124.8 0.0 all-gather.3.cloned.1.call-start
  124.8 74.7 %reduce-scatter.4.cloned.1.call-done = f32[640,768]{1,0:T(8,128)} async-done(((f32[2560,768]{1,0:T(8,128)}), f32[640,768]{1,0:T(8,128)}) %reduce-scatter.4.cloned.1.call-update) | async-done | bytes 1966096 | tf_op jit(solution)/shard_map/reduce_scatter | solution.py:230
  199.5 0.0 copy-done.1
  199.5 3.3 fusion.17
  202.9 0.0 all-gather.3.cloned.1.call-update
  202.9 0.0 reduce-scatter.8.cloned.1.call-start
  202.9 7.3 %fusion.23 = f32[2560,192]{0,1:T(8,128)} fusion(bf16[2560,1536]{1,0:T(8,128)(2,1)} %bitcast.17, bf16[192,1536]{1,0:T(8,128)(2,1)} %param.13), kind=kOutput, calls=%fused_computation.31 | convolution fusion | flops 1509949440 | bytes 10420224 | tf_op jit(solution)/shard_map/dot_general | solution.py:29
  210.2 0.0 reduce-scatter.8.cloned.1.call-update
  210.2 0.0 all-gather.5.cloned.1.call-start
  210.3 0.5 all-gather.5.cloned.1.call-update
  210.8 0.0 reduce-scatter.6.cloned.1.call-start
  210.8 37.0 %all-gather.3.cloned.1.call-done = bf16[2560,768]{1,0:T(8,128)(2,1)} async-done(((bf16[640,768]{1,0:T(8,128)(2,1)}), bf16[2560,768]{1,0:T(8,128)(2,1)}) %all-gather.3.cloned.1.call-update) | async-done | bytes 3932176 | tf_op jit(solution)/shard_map/all_gather | solution.py:235
  247.9 0.0 copy-done
  247.9 11.3 %fusion.22 = f32[2560,1536]{1,0:T(8,128)} fusion(bf16[2560,768]{1,0:T(8,128)(2,1)} %all-gather.3.cloned.1.call-done, bf16[1536,768]{1,0:T(8,128)(2,1)S(1)} %copy-done), kind=kOutput, calls=%fused_computation.30 | convolution fusion | flops 6039797760 | bytes 22020096 | tf_op jit(solution)/shard_map/dot_general | solution.py:29
  259.2 0.0 reduce-scatter.6.cloned.1.call-update
  259.2 0.9 copy-done.2
  260.2 15.6 %all_gather.11 = bf16[2560,192]{0,1:T(8,128)(2,1)S(1)} all-gather(bf16[640,192]{0,1:T(8,128)(2,1)S(1)} %copy-done.2), channel_id=1, replica_groups=mesh['gx'=8,'gy'=4,'gz'=4] {'gz'}, dimensions={0}, use_global_device_ids=true | all-gather | bytes 1228800 | tf_op jit(solution)/shard_map/all_gather | solution.py:224
  275.8 5.9 fusion.9
  281.7 3.0 reduce-scatter.8.cloned.1.call-done
  284.7 1.8 convert_element_type.33
  286.4 44.6 %all-gather.5.cloned.1.call-done = bf16[2560,768]{1,0:T(8,128)(2,1)} async-done(((bf16[640,768]{1,0:T(8,128)(2,1)}), bf16[2560,768]{1,0:T(8,128)(2,1)}) %all-gather.5.cloned.1.call-update) | async-done | bytes 3932176 | tf_op jit(solution)/shard_map/all_gather | solution.py:223
  331.1 11.6 %multiply_convert_fusion = bf16[768,1536]{1,0:T(8,128)(2,1)} fusion(bf16[2560,1536]{1,0:T(8,128)(2,1)} %bitcast.19, bf16[2560,768]{1,0:T(8,128)(2,1)} %all-gather.5.cloned.1.call-done), kind=kOutput, calls=%fused_computation.6 | convolution fusion | flops 6053953536 | bytes 14155776 | tf_op jit(solution)/shard_map/dot_general | solution.py:23
  342.6 0.0 copy-done.3
  342.7 9.8 %multiply_convert_fusion.1 = bf16[1536,768]{1,0:T(8,128)(2,1)} fusion(bf16[2560,1536]{1,0:T(8,128)(2,1)} %bitcast.15, bf16[2560,768]{1,0:T(8,128)(2,1)S(1)} %copy-done.3), kind=kOutput, calls=%fused_computation.7 | convolution fusion | flops 6042157056 | bytes 14155776 | tf_op jit(solution)/shard_map/dot_general | solution.py:23
  352.5 249.4 %reduce-scatter.6.cloned.1.call-done = f32[80,1536]{1,0:T(8,128)} async-done(((f32[2560,1536]{1,0:T(8,128)}), f32[80,1536]{1,0:T(8,128)}) %reduce-scatter.6.cloned.1.call-update) | async-done | bytes 491536 | tf_op jit(solution)/shard_map/reduce_scatter | solution.py:240
  601.9 1.7 convert_element_type.32
  (2 shorter events, 0.0 us)
Async XLA Ops:
  7.2 240.7 %copy-start = (bf16[1536,768]{1,0:T(8,128)(2,1)S(1)}, bf16[1536,768]{1,0:T(8,128)(2,1)}, u32[]{:S(2)}) copy-start(bf16[1536,768]{1,0:T(8,128)(2,1)} %param.11) | copy-start | bytes 7077892
  7.2 192.3 %reduce-scatter.4.cloned.1.call-start = ((), (), s32[]{:S(2)}) async-start(), calls=%async_computation.3 | async-start | bytes 9830400 | tf_op jit(solution)/shard_map/reduce_scatter | solution.py:230
  124.8 74.7 %copy-start.1 = (bf16[640,768]{1,0:T(8,128)(2,1)S(1)}, bf16[640,768]{1,0:T(8,128)(2,1)}, u32[]{:S(2)}) copy-start(bf16[640,768]{1,0:T(8,128)(2,1)} %param.9) | copy-start | bytes 2949124
  124.8 123.1 %all-gather.3.cloned.1.call-start = ((), (), s32[]{:S(2)}) async-start(), calls=%async_computation.4 | async-start | bytes 4915200 | tf_op jit(solution)/shard_map/all_gather | solution.py:235
  202.9 81.8 %reduce-scatter.8.cloned.1.call-start = ((), (), s32[]{:S(2)}) async-start(), calls=%async_computation.6 | async-start | bytes 2457600 | tf_op jit(solution)/shard_map/reduce_scatter | solution.py:244
  210.2 120.9 %all-gather.5.cloned.1.call-start = ((), (), s32[]{:S(2)}) async-start(), calls=%async_computation.7 | async-start | bytes 4915200 | tf_op jit(solution)/shard_map/all_gather | solution.py:223
  210.8 391.1 %reduce-scatter.6.cloned.1.call-start = ((), (), s32[]{:S(2)}) async-start(), calls=%async_computation.5 | async-start | bytes 16220160 | tf_op jit(solution)/shard_map/reduce_scatter | solution.py:240
  259.2 0.9 copy-start.2
  331.1 11.6 %copy-start.3 = (bf16[2560,768]{1,0:T(8,128)(2,1)S(1)}, bf16[2560,768]{1,0:T(8,128)(2,1)}, u32[]{:S(2)}) copy-start(bf16[2560,768]{1,0:T(8,128)(2,1)} %all-gather.3.cloned.1.call-done) | copy-start | bytes 11796484
Sparse Core Ops, SparseCore 0:
  124.9 74.5 reduce-scatter.3
  203.0 44.8 all-gather.2
  250.9 33.7 reduce-scatter.7
  286.2 44.8 all-gather.4
  336.4 265.4 reduce-scatter.5

commit v2 on v1

v2 whole, which is shorter than its diff:
```python
import math

import jax
import jax.numpy as jnp
from jax import lax
from jax.experimental import pallas as pl
from jax.experimental.pallas import tpu as pltpu
from jax.sharding import PartitionSpec as P

MESH = pl.DeviceIdType.MESH
f32, bf16 = jnp.float32, jnp.bfloat16
inv_root_two = 0.7071067811865476
inv_root_two_pi = 0.3989422804014327
SEMS = 320


def nt(left, right):
    return lax.dot_general(left, right, (((1,), (1,)), ((), ())), preferred_element_type=f32)


def tn(left, right):
    return lax.dot_general(left, right, (((0,), (0,)), ((), ())), preferred_element_type=f32)


class Place:
    def __init__(self, block):
        gx, gy, gz = (lax.axis_index(a) for a in ("gx", "gy", "gz"))
        self.block = block
        self.z, self.yh, self.x, self.gz = gx // 2, lax.rem(gx, 2), gy, gz
        self.yl, self.c = gz // 2, lax.rem(gz, 2)
        z, yh, x = self.z, self.yh, self.x
        zp, zm, z2 = (lax.rem(z + k, 4) for k in (1, 3, 2))
        xp, xm, x2 = (lax.rem(x + k, 4) for k in (1, 3, 2))
        self.zs = (z, zp, zm, z2)
        self.xs = (x, xp, xm, x2)
        self.dev = {
            "x+": (gx, xp, gz),
            "x-": (gx, xm, gz),
            "z+": (zp * 2 + yh, x, gz),
            "z-": (zm * 2 + yh, x, gz),
            "yh": (z * 2 + 1 - yh, x, gz),
            "yl": (gx, gy, (1 - self.yl) * 2 + self.c),
            "c": (gx, gy, self.yl * 2 + 1 - self.c),
        }

    def rows(self, z, yh, x):
        return pl.ds(pl.multiple_of((z * 8 + yh * 4 + x) * self.block, self.block), self.block)

    def chunk(self, z, yh):
        n = 4 * self.block
        return pl.ds(pl.multiple_of((z * 2 + yh) * n, n), n)

    def shard(self, j):
        n = 8 * self.block
        return pl.ds(pl.multiple_of(j * n, n), n)


class Links:
    def __init__(self, place, send_sems, recv_sems):
        self.place, self.ss, self.rs = place, send_sems, recv_sems
        self.names, self.started = {}, []

    def copy(self, key, src, dst, to):
        i = self.names.setdefault(key, len(self.names))
        return pltpu.make_async_remote_copy(
            src_ref=src, dst_ref=dst, send_sem=self.ss.at[i], recv_sem=self.rs.at[i],
            device_id=self.place.dev[to], device_id_type=MESH)

    def send(self, key, src, dst, to):
        c = self.copy(key, src, dst, to)
        c.start()
        self.started.append(c)

    def got(self, key, view):
        self.copy(key, view, view, "x+").wait_recv()

    def sent(self):
        for c in self.started:
            c.wait_send()
        self.started = []


class Gather:
    def __init__(self, name, full, place, links):
        self.name, self.full, self.p, self.l = name, full, place, links
        self.first = (("x+", "x-"), ("z+", "z-"))
        self.second = (("z+", "z-"), ("x+", "x-"))
        self.one = (place.xs, place.zs)
        self.two = (place.zs, place.xs)

    def view(self, part, yy, i, j, half=None):
        zz, xx = (j, i) if part == 0 else (i, j)
        width = self.full.shape[-1] // 2
        start, n = part * width, width
        if half is not None:
            n = width // 2
            start += half * n
        return self.full.at[self.p.rows(zz, yy, xx), pl.ds(start, n)]

    def send(self, key, view, to):
        self.l.send((self.name,) + key, view, view, to)

    def got(self, key, view):
        self.l.got((self.name,) + key, view)

    def exchange(self):
        own = self.full.at[self.p.rows(self.p.z, self.p.yh, self.p.x)]
        self.send(("y",), own, "yh")

    def exchanged(self):
        self.got(("y",), self.full.at[self.p.rows(self.p.z, 1 - self.p.yh, self.p.x)])

    def r0(self, w, yy):
        for key, ways in (("f", self.first), ("s0", self.second)):
            for p in (0, 1):
                own = self.view(p, yy, self.one[p][0], self.two[p][0])
                for s in (0, 1):
                    self.send((w, p, key, s), own, ways[p][s])

    def r1(self, w, yy):
        for p in (0, 1):
            i0, ip, im, i2 = self.one[p]
            j0 = self.two[p][0]
            self.got((w, p, "f", 0), self.view(p, yy, im, j0))
            self.send((w, p, "ff", 0), self.view(p, yy, im, j0, 0), self.first[p][0])
            self.got((w, p, "f", 1), self.view(p, yy, ip, j0))
            self.send((w, p, "ff", 1), self.view(p, yy, ip, j0, 1), self.first[p][1])
        for p in (0, 1):
            i0, ip, im, i2 = self.one[p]
            j0 = self.two[p][0]
            for k, i in (("s1", im), ("s2", ip)):
                for s in (0, 1):
                    self.send((w, p, k, s), self.view(p, yy, i, j0), self.second[p][s])

    def r2(self, w, yy):
        for p in (0, 1):
            i2, j0 = self.one[p][3], self.two[p][0]
            for h in (0, 1):
                self.got((w, p, "ff", h), self.view(p, yy, i2, j0, h))
            for s in (0, 1):
                self.send((w, p, "s3", s), self.view(p, yy, i2, j0), self.second[p][s])

    def order(self, p, k):
        i0, ip, im, i2 = self.one[p]
        return (i0, im, ip, i2)[k]

    def r3(self, w, yy, k):
        for p in (0, 1):
            i = self.order(p, k)
            j0, jp, jm, j2 = self.two[p]
            self.got((w, p, f"s{k}", 0), self.view(p, yy, i, jm))
            self.send((w, p, f"sf{k}", 0), self.view(p, yy, i, jm, 0), self.second[p][0])
            self.got((w, p, f"s{k}", 1), self.view(p, yy, i, jp))
            self.send((w, p, f"sf{k}", 1), self.view(p, yy, i, jp, 1), self.second[p][1])

    def r4(self, w, yy, k):
        for p in (0, 1):
            i, j2 = self.order(p, k), self.two[p][3]
            for h in (0, 1):
                self.got((w, p, f"sf{k}", h), self.view(p, yy, i, j2, h))


class Scatter:
    def __init__(self, part_sums, far1, near1, far2, near2, keep, place, links):
        self.d, self.far1, self.near1, self.far2, self.near2, self.keep = part_sums, far1, near1, far2, near2, keep
        self.p, self.l = place, links
        self.first = (("z+", "z-"), ("x+", "x-"))
        self.second = (("x+", "x-"), ("z+", "z-"))
        self.one = (place.zs, place.xs)
        self.two = (place.xs, place.zs)
        self.width = part_sums.shape[-1] // 2

    def view(self, part, yy, i, j, half=None):
        zz, xx = (i, j) if part == 0 else (j, i)
        start, n = part * self.width, self.width
        if half is not None:
            n = self.width // 2
            start += half * n
        return self.d.at[self.p.rows(zz, yy, xx), pl.ds(start, n)]

    def order(self, p, k):
        j0, jp, jm, j2 = self.two[p]
        return (j2, jp, jm, j0)[k]

    def s1(self, w, yy, p):
        for k in range(4):
            for h in (0, 1):
                self.l.send(("rs", w, p, "far1", k, h), self.view(p, yy, self.one[p][3], self.order(p, k), h),
                            self.far1.at[w, p, k, h], self.first[p][h])

    def fold(self, into, *terms):
        total = into[...].astype(f32)
        for t in terms:
            total = total + t[...].astype(f32)
        into[...] = total.astype(into.dtype)

    def s2(self, w, yy, k):
        for p in (0, 1):
            j = self.order(p, k)
            for h in (0, 1):
                i = self.one[p][1 + h]
                self.l.got(("rs", w, p, "far1", k, h), self.far1.at[w, p, k, h])
                self.fold(self.view(p, yy, i, j, h), self.far1.at[w, p, k, h])
                self.l.send(("rs", w, p, "near1", k, h), self.view(p, yy, i, j), self.near1.at[w, p, k, h], self.first[p][h])

    def s3(self, w, yy, k):
        for p in (0, 1):
            for h in (0, 1):
                self.l.got(("rs", w, p, "near1", k, h), self.near1.at[w, p, k, h])
            mine = self.view(p, yy, self.one[p][0], self.order(p, k))
            if k == 3:
                self.keep[w, p] = (mine[...].astype(f32) + self.near1[w, p, k, 0].astype(f32)
                                   + self.near1[w, p, k, 1].astype(f32))
            else:
                self.fold(mine, self.near1.at[w, p, k, 0], self.near1.at[w, p, k, 1])
            if k == 0:
                for h in (0, 1):
                    self.l.send(("rs", w, p, "far2", h), self.view(p, yy, self.one[p][0], self.order(p, k), h),
                                self.far2.at[w, p, h], self.second[p][h])

    def t2(self, w, yy):
        for p in (0, 1):
            for h in (0, 1):
                into = self.view(p, yy, self.one[p][0], self.two[p][1 + h], h)
                self.l.got(("rs", w, p, "far2", h), self.far2.at[w, p, h])
                self.fold(into, self.far2.at[w, p, h])
                self.l.send(("rs", w, p, "near2", h), self.view(p, yy, self.one[p][0], self.two[p][1 + h]),
                            self.near2.at[w, p, h], self.second[p][h])

    def t3(self, w, p):
        for h in (0, 1):
            self.l.got(("rs", w, p, "near2", h), self.near2.at[w, p, h])
        return self.keep[w, p] + self.near2[w, p, 0].astype(f32) + self.near2[w, p, 1].astype(f32)


def kernel(scale, n_in, c_in, h_in, g_in, wi_in, wo_in, wp_in,
           gn_out, gc_out, gwi_out, gwo_out, gwp_out,
           G, N, ACT, CTX, HP, WIN, WOUT, WPROJ, GH, SLOPE, P1S, P1R, POWN, P2S, P2R,
           C1S, C1R, COWN, C2S, C2R, FAR1, NEAR1, FAR2, NEAR2, KEEP, YS, YR, GN, GC, ss, rs, ls):
    block = g_in.shape[0]
    p = Place(block)
    z, yh, x, gz, yl, c = p.z, p.yh, p.x, p.gz, p.yl, p.c
    o = 1 - yh
    chunk_rows = 4 * block

    bar = pltpu.get_barrier_semaphore()
    for d in p.dev.values():
        pl.semaphore_signal(bar, inc=1, device_id=d, device_id_type=MESH)
    loads = {}
    for i, (name, src, dst) in enumerate((
            ("g", g_in, G.at[p.rows(z, yh, x)]), ("h", h_in, HP), ("c", c_in, CTX.at[p.shard(gz)]),
            ("n", n_in, N.at[p.rows(z, yh, x)]), ("wo", wo_in, WOUT), ("wp", wp_in, WPROJ), ("wi", wi_in, WIN))):
        loads[name] = pltpu.make_async_copy(src, dst, ls.at[i])
        loads[name].start()
    stores = []

    def store(src, dst):
        s = pltpu.make_async_copy(src, dst, ls.at[8 + len(stores)])
        s.start()
        stores.append(s)

    pl.semaphore_wait(bar, len(p.dev))

    gl, nl, yl_links, rl = (Links(p, ss, rs) for _ in range(4))
    for other in (nl, yl_links, rl):
        other.names = gl.names
    a, b = Gather("g", G, p, gl), Gather("n", N, p, nl)
    red = Scatter(G, FAR1, NEAR1, FAR2, NEAR2, KEEP, p, rl)
    wave_yh = (yh, o)

    def spread(name, view):
        yl_links.send((name, "y"), view, view, "yl")
        yl_links.send((name, "c"), view, view, "c")

    def relay(name, view_of):
        v = view_of((1 - yl) * 2 + c)
        yl_links.got((name, "y"), v)
        yl_links.send((name, "cy"), v, v, "c")

    def spread_done(name, view_of):
        yl_links.got((name, "c"), view_of(yl * 2 + 1 - c))
        yl_links.got((name, "cy"), view_of((1 - yl) * 2 + 1 - c))

    act_rows = lambda j: ACT.at[p.shard(j)]
    ctx_rows = lambda j: CTX.at[p.shard(j)]

    def gh_rows(w):
        return lambda j: GH.at[p.chunk(j, wave_yh[w])]

    def act_peer(w):
        for s, yy in enumerate((1 - yl, yl)):
            P1S[w, s] = nt(G[p.chunk(yy * 2 + 1 - c, wave_yh[w]), :], WOUT[...])
            yl_links.send(("p1", w, s), P1S.at[w, s], P1R.at[w, s], "c")

    def act_own(w):
        yl_links.got(("p1", w, 0), P1R.at[w, 0])
        P2S[w] = (nt(G[p.chunk((1 - yl) * 2 + c, wave_yh[w]), :], WOUT[...]) + P1R[w, 0]).astype(bf16)
        yl_links.send(("p2", w), P2S.at[w], P2R.at[w], "yl")
        yl_links.got(("p1", w, 1), P1R.at[w, 1])
        POWN[w] = nt(G[p.chunk(gz, wave_yh[w]), :], WOUT[...]) + P1R[w, 1]

    def hidden(w):
        yl_links.got(("p2", w), P2R.at[w])
        n = chunk_rows
        local = pl.ds(pl.multiple_of(wave_yh[w] * n, n), n)
        GH[p.chunk(gz, wave_yh[w]), :] = ((POWN[w] + P2R[w].astype(f32)) * SLOPE[local, :]).astype(bf16)
        spread(("gh", w), gh_rows(w)(gz))

    def ctx_peer():
        for s, yy in enumerate((1 - yl, yl)):
            C1S[s] = nt(G[p.shard(yy * 2 + 1 - c), :], WPROJ[...])
            yl_links.send(("c1", s), C1S.at[s], C1R.at[s], "c")

    def ctx_own():
        yl_links.got(("c1", 0), C1R.at[0])
        C2S[...] = (nt(G[p.shard((1 - yl) * 2 + c), :], WPROJ[...]) + C1R[0]).astype(bf16)
        yl_links.send(("c2",), C2S, C2R, "yl")
        yl_links.got(("c1", 1), C1R.at[1])
        COWN[...] = nt(G[p.shard(gz), :], WPROJ[...]) + C1R[1]

    def ctx_done():
        yl_links.got(("c2",), C2R)
        GC[...] = (COWN[...] + C2R[...].astype(f32)).astype(bf16)
        store(GC, gc_out)

    def w_out_tiles(f):
        @pl.loop(0, 3)
        def _(i):
            cols = pl.ds(pl.multiple_of(i * 512, 512), 512)
            WOUT[pl.ds(f * 256, 256), cols] = (tn(ACT[:, pl.ds(f * 256, 256)], G[:, cols]) * scale).astype(bf16)

    def w_proj_tiles():
        @pl.loop(0, 3)
        def _(i):
            cols = pl.ds(pl.multiple_of(i * 512, 512), 512)
            WPROJ[:, cols] = (tn(CTX[...], G[:, cols]) * scale).astype(bf16)

    def w_in_tiles(start, count):
        @pl.loop(start, start + count)
        def _(i):
            cols = pl.ds(pl.multiple_of(i * 256, 256), 256)
            WIN2[cols, :] = (tn(N[:, cols], GH[...]) * scale).astype(bf16)

    def partial(yy, zz):
        G[p.chunk(zz, yy), :] = nt(GH[p.chunk(zz, yy), :], WIN[...]).astype(bf16)

    def partials(w, yy):
        z0, zp, zm, z2 = p.zs
        partial(yy, z2)
        red.s1(w, yy, 0)

        @pl.loop(0, 3)
        def _(i):
            partial(yy, lax.rem(z2 + 1 + i, 4))

        red.s1(w, yy, 1)

    WIN2 = WIN

    loads["g"].wait()
    a.exchange()
    a.r0(0, yh)
    loads["c"].wait()
    spread("ctx", ctx_rows(gz))
    loads["h"].wait()

    @pl.loop(0, HP.shape[0] // 16)
    def _(i):
        here = pl.ds(pl.multiple_of(i * 16, 16), 16)
        v = HP[here, :].astype(f32)
        cdf = 0.5 * (1.0 + lax.erf(v * inv_root_two))
        density = jnp.exp(-0.5 * v * v) * inv_root_two_pi
        SLOPE[here, :] = cdf + v * density
        ACT[pl.ds(pl.multiple_of(gz * HP.shape[0] + i * 16, 16), 16), :] = (v * cdf).astype(bf16)

    spread("act", act_rows(gz))
    a.r1(0, yh)
    a.r3(0, yh, 0)
    a.r2(0, yh)
    a.exchanged()
    a.r0(1, o)
    a.r3(0, yh, 1)
    a.r3(0, yh, 2)
    a.r1(1, o)
    a.r3(0, yh, 3)
    a.r3(1, o, 0)
    a.r2(1, o)
    loads["n"].wait()
    b.exchange()
    for j in range(4):
        a.r4(0, yh, j)
    b.r0(0, yh)
    loads["wo"].wait()
    act_peer(0)
    a.r3(1, o, 1)
    act_own(0)
    a.r3(1, o, 2)
    relay("ctx", ctx_rows)
    b.r1(0, yh)
    a.r3(1, o, 3)
    b.r3(0, yh, 0)
    b.r2(0, yh)
    relay("act", act_rows)
    for j in range(4):
        a.r4(1, o, j)
    b.exchanged()
    b.r0(1, o)
    act_peer(1)
    b.r3(0, yh, 1)
    act_own(1)
    hidden(0)
    b.r3(0, yh, 2)
    b.r1(1, o)
    loads["wp"].wait()
    ctx_peer()
    b.r3(0, yh, 3)
    b.r3(1, o, 0)
    b.r2(1, o)
    ctx_own()
    spread_done("act", act_rows)
    w_out_tiles(0)
    for j in range(4):
        b.r4(0, yh, j)
    relay(("gh", 0), gh_rows(0))
    hidden(1)
    b.r3(1, o, 1)
    w_out_tiles(1)
    b.r3(1, o, 2)
    w_out_tiles(2)
    store(WOUT, gwo_out)
    b.r3(1, o, 3)
    spread_done("ctx", ctx_rows)
    w_proj_tiles()
    store(WPROJ, gwp_out)
    gl.sent()
    loads["wi"].wait()
    relay(("gh", 1), gh_rows(1))
    spread_done(("gh", 1), gh_rows(1))
    partials(0, o)
    for j in range(4):
        b.r4(1, o, j)
    spread_done(("gh", 0), gh_rows(0))
    red.s2(0, o, 0)
    red.s2(0, o, 1)
    partials(1, yh)
    red.s2(0, o, 2)
    red.s2(0, o, 3)
    ctx_done()
    red.s3(0, o, 0)
    red.s2(1, yh, 0)
    red.s3(0, o, 1)
    red.s3(0, o, 2)
    red.s2(1, yh, 1)
    red.t2(0, o)
    red.s3(0, o, 3)
    red.s2(1, yh, 2)
    red.s2(1, yh, 3)
    w_in_tiles(0, 2)
    for q in (0, 1):
        YS[:, pl.ds(q * red.width, red.width)] = red.t3(0, q)
    yl_links.send(("yh",), YS, YR, "yh")
    red.s3(1, yh, 0)
    w_in_tiles(2, 1)
    red.s3(1, yh, 1)
    red.s3(1, yh, 2)
    red.t2(1, yh)
    red.s3(1, yh, 3)
    w_in_tiles(3, 3)
    store(WIN2, gwi_out)
    yl_links.got(("yh",), YR)
    for q in (0, 1):
        cols = pl.ds(q * red.width, red.width)
        GN[:, cols] = (red.t3(1, q) + YR[:, cols]).astype(bf16)
    store(GN, gn_out)
    for links in (nl, yl_links, rl):
        links.sent()
    for s in stores:
        s.wait()


def body(normed, context, hidden_pre, grad_out, w_in, w_out, w_proj):
    block, width = grad_out.shape
    shard, hidden = hidden_pre.shape
    feats = context.shape[1]
    tokens = 32 * block
    chunk = 4 * block
    half = width // 2
    scratch = [
        pltpu.VMEM((tokens, width), bf16),
        pltpu.VMEM((tokens, width), bf16),
        pltpu.VMEM((tokens, hidden), bf16),
        pltpu.VMEM((tokens, feats), bf16),
        pltpu.VMEM((shard, hidden), bf16),
        pltpu.VMEM(w_in.shape, bf16),
        pltpu.VMEM(w_out.shape, bf16),
        pltpu.VMEM(w_proj.shape, bf16),
        pltpu.VMEM((tokens, hidden), bf16),
        pltpu.VMEM((shard, hidden), f32),
        pltpu.VMEM((2, 2, chunk, hidden), f32),
        pltpu.VMEM((2, 2, chunk, hidden), f32),
        pltpu.VMEM((2, chunk, hidden), f32),
        pltpu.VMEM((2, chunk, hidden), bf16),
        pltpu.VMEM((2, chunk, hidden), bf16),
        pltpu.VMEM((2, shard, feats), f32),
        pltpu.VMEM((2, shard, feats), f32),
        pltpu.VMEM((shard, feats), f32),
        pltpu.VMEM((shard, feats), bf16),
        pltpu.VMEM((shard, feats), bf16),
        pltpu.VMEM((2, 2, 4, 2, block, half // 2), bf16),
        pltpu.VMEM((2, 2, 4, 2, block, half), bf16),
        pltpu.VMEM((2, 2, 2, block, half // 2), bf16),
        pltpu.VMEM((2, 2, 2, block, half), bf16),
        pltpu.VMEM((2, 2, block, half), f32),
        pltpu.VMEM((block, width), f32),
        pltpu.VMEM((block, width), f32),
        pltpu.VMEM((block, width), bf16),
        pltpu.VMEM((shard, feats), bf16),
        pltpu.SemaphoreType.DMA((SEMS,)),
        pltpu.SemaphoreType.DMA((SEMS,)),
        pltpu.SemaphoreType.DMA((16,)),
    ]
    outs = [normed, context, w_in, w_out, w_proj]

    def call(*refs):
        kernel(1.0 / math.sqrt(tokens), *refs)

    return tuple(pl.pallas_call(
        call,
        out_shape=[jax.ShapeDtypeStruct(v.shape, v.dtype) for v in outs],
        in_specs=[pl.BlockSpec(memory_space=pl.ANY)] * 7,
        out_specs=[pl.BlockSpec(memory_space=pl.ANY)] * 5,
        scratch_shapes=scratch,
        compiler_params=pltpu.CompilerParams(
            collective_id=0, has_side_effects=True, vmem_limit_bytes=63 * 2**20),
    )(normed, context, hidden_pre, grad_out, w_in, w_out, w_proj))


def solution(mesh):
    in_specs = (
        P(("gx", "gy"), "gz"),
        P("gz", ("gx", "gy")),
        P("gz", ("gx", "gy")),
        P(("gx", "gy"), "gz"),
        P("gz", ("gx", "gy")),
        P(("gx", "gy"), "gz"),
        P(("gx", "gy"), "gz"),
    )
    out_specs = (
        P(("gx", "gy"), "gz"),
        P("gz", ("gx", "gy")),
        P("gz", ("gx", "gy")),
        P(("gx", "gy"), "gz"),
        P(("gx", "gy"), "gz"),
    )
    return jax.shard_map(body, mesh=mesh, in_specs=in_specs, out_specs=out_specs, check_vma=False)
```

time: 610 us -> 176 us (0.29)
  waiting for transfers between devices: 409 us -> 0 us
  Pallas kernels: 106 us -> 164 us
  matrix products: 57.1 us -> 0 us
  blocking collectives: 15.6 us -> 0 us
  between operations: 13.8 us -> 0.64 us
  local copies, waits for them, and re-layouts: 0.94 us -> 11 us
  other arithmetic: 6.85 us -> 0 us
    reduce_scatter x3 -> x0, waiting for transfers between devices: 327 us -> none  [the longest x1 249 us: body(): lax.psum_scatter(contract_cols(panel, w_in), ('gx', 'gy'), scatter_dimens...]
    all_gather x2 -> x0, waiting for transfers between devices: 81.7 us -> none  [the longest x1 44.6 us: body(): lax.all_gather(hidden_pre, 'gz', axis=0, tiled=True)]
    pallas_call x1, Pallas kernels: 106 us -> 164 us  [body(): pl.pallas_call(call, out_shape=[jax.ShapeDtypeStruct(v.shape, v.dtype) fo...]
    dot_general x6 -> x0, matrix products: 57.1 us -> none  [the longest x3 29.9 us: contract_cols(): lax.dot_general(left, right, (((1,), (1,)), ((), ())), preferred_element_...]
    all_gather x1 -> x0, blocking collectives: 15.6 us -> none  [body(): lax.all_gather(context, 'gz', axis=0, tiled=True)]
    unnamed x8 -> x9, local copies, waits for them, and re-layouts: 0.94 us -> 9.15 us
    convert_element_type x3 -> x0, other arithmetic: 6.85 us -> none  [the longest x1 3.35 us: body(): hidden_share = (grad_share * local_slope).astype(jnp.bfloat16)]
  transfers between devices with their start and end apart: 5 -> 0, of which waited for: 5 -> 0; matrix products, arithmetic and copies ran while one was open for 8% -> 0% of each run, Pallas kernels for 0% -> 0%
where the time goes in v2:
time: 176 us
  Pallas kernels  164 us (93%)
  local copies, waits for them, and re-layouts  11 us (6%)
    pallas_call x1, Pallas kernels, body(): pl.pallas_call(call, out_shape=[jax.ShapeDtypeStruct(v.shape, v.dtype) fo...  164 us
    unnamed x9, local copies, waits for them, and re-layouts  9.15 us

profile of v2, /device:TPU:0, one launch (start us, length us, event | category | flops | bytes accessed | tf_op | source)
XLA Modules:
  0.0 175.8 jit_solution(3642591154565003437)
XLA Ops:
  0.6 1.8 %copy.12.refs_1_ = bf16[640,192]{1,0:T(8,128)(2,1)} copy(bf16[640,192]{0,1:T(8,128)(2,1)} %param.8) | data formatting | bytes 491520 | tf_op args[1]
  2.5 164.2 %shard_map.110 = (bf16[80,1536]{1,0:T(8,128)(2,1)}, bf16[640,192]{1,0:T(8,128)(2,1)}, bf16[1536,768]{1,0:T(8,128)(2,1)}, bf16[768,1536]{1,0:T(8,128)(2,1)}, bf16[192,1536]{1,0:T(8,128)(2,1)}) custom-call(bf16[80,1536]{1,0:T(8,128)(2,1)} %refs_0_.1, bf16[640,192]{1,0:T(8,128)(2,1)} %copy.12.refs_1_, bf16[640,768]{1,0:T(8,128)(2,1)} %refs_2_.1, ...), custom_call_target="tpu_custom_call" | custom-call | tf_op jit(solution)/shard_map/pallas_call | solution.py:527
  166.7 1.8 %copy.13 = bf16[640,192]{0,1:T(8,128)(2,1)} copy(bf16[640,192]{1,0:T(8,128)(2,1)} %get-tuple-element.6) | data formatting | bytes 491520 | tf_op jit(solution)/shard_map/pallas_call | solution.py:527
  168.5 1.7 copy.18
  170.2 0.0 copy-start
  170.2 3.4 %copy.19 = bf16[1536,768]{1,0:T(8,128)(2,1)} copy(bf16[1536,768]{1,0:T(8,128)(2,1)} %get-tuple-element.17) | data formatting | bytes 4718592
  173.6 0.0 copy-done
  173.6 0.0 copy-start.1
  173.6 1.4 copy.20
  175.0 0.1 copy-done.1
  175.0 0.8 copy.21
Async XLA Ops:
  170.2 3.4 %copy-start = (bf16[768,1536]{1,0:T(8,128)(2,1)S(1)}, bf16[768,1536]{1,0:T(8,128)(2,1)}, u32[]{:S(2)}) copy-start(bf16[768,1536]{1,0:T(8,128)(2,1)} %get-tuple-element.18) | copy-start | bytes 7077892
  173.6 1.5 copy-start.1

commit v3 on v0

v3 whole, which is shorter than its diff:
```python
import math

import jax
import jax.numpy as jnp
from jax import lax
from jax.experimental import pallas as pl
from jax.experimental.pallas import tpu as pltpu
from jax.sharding import PartitionSpec as P

MESH = pl.DeviceIdType.MESH
f32, bf16 = jnp.float32, jnp.bfloat16
inv_root_two = 0.7071067811865476
inv_root_two_pi = 0.3989422804014327
SEMS = 352
K = dict(g=(1e9, 2.5), n=(2.5, 2.5), nx=(1, (("gh", 0, 1, "spread"),), 1e9), act=12, ctx=13, rs=(1e9, 1.0), ab=0.5, pieces=4)


def nt(left, right):
    return lax.dot_general(left, right, (((1,), (1,)), ((), ())), preferred_element_type=f32)


def nn(left, right):
    return lax.dot_general(left, right, (((1,), (0,)), ((), ())), preferred_element_type=f32)


def tn(left, right):
    return lax.dot_general(left, right, (((0,), (0,)), ((), ())), preferred_element_type=f32)


class Place:
    def __init__(self, block):
        gx, gy, gz = (lax.axis_index(a) for a in ("gx", "gy", "gz"))
        self.block = block
        self.z, self.yh, self.x, self.gz = gx // 2, lax.rem(gx, 2), gy, gz
        self.yl, self.c = gz // 2, lax.rem(gz, 2)
        z, yh, x = self.z, self.yh, self.x
        zp, zm, z2 = (lax.rem(z + k, 4) for k in (1, 3, 2))
        xp, xm, x2 = (lax.rem(x + k, 4) for k in (1, 3, 2))
        self.zs = (z, zp, zm, z2)
        self.xs = (x, xp, xm, x2)
        self.dev = {
            "x+": (gx, xp, gz),
            "x-": (gx, xm, gz),
            "z+": (zp * 2 + yh, x, gz),
            "z-": (zm * 2 + yh, x, gz),
            "yh": (z * 2 + 1 - yh, x, gz),
            "yl": (gx, gy, (1 - self.yl) * 2 + self.c),
            "c": (gx, gy, self.yl * 2 + 1 - self.c),
        }

    def rows(self, z, yh, x):
        return pl.ds(pl.multiple_of((z * 8 + yh * 4 + x) * self.block, self.block), self.block)

    def chunk(self, z, yh):
        n = 4 * self.block
        return pl.ds(pl.multiple_of((z * 2 + yh) * n, n), n)

    def shard(self, j):
        n = 8 * self.block
        return pl.ds(pl.multiple_of(j * n, n), n)


class Plan:
    rate = {"x+": 46e3, "x-": 46e3, "z+": 46e3, "z-": 46e3, "y": 46e3, "c": 6e5}
    latency = 1.5

    def __init__(self, place, send_sems, recv_sems):
        self.place, self.ss, self.rs = place, send_sems, recv_sems
        self.tasks, self.index, self.recv, self.local = {}, {}, {}, {}
        self.done, self.copies = set(), {}

    def load(self, key, copy, at):
        copy.start()
        self.local[key] = (copy, at)

    def add(self, name, prio, fn=None, needs=(), after=(), sends=(), dur=0.1, backlog=1e9):
        self.tasks[name] = (prio, fn, tuple(needs), tuple(after), tuple(sends), dur, backlog)
        for key, src, dst, to, here in sends:
            self.index[key] = len(self.index)
            self.recv[key] = here

    def order(self):
        arrive = {k: at for k, (_, at) in self.local.items()}
        free = dict.fromkeys(self.rate, 0.0)
        left, finished, now, out = dict(self.tasks), set(), 0.0, []
        self.log = []
        while left:
            ready, times = [], []
            for name, (prio, fn, needs, after, sends, dur, backlog) in left.items():
                if any(a not in finished for a in after) or any(k not in arrive for k in needs):
                    continue
                at = max([arrive[k] for k in needs], default=0.0)
                for s in sends:
                    at = max(at, free[self.link(s[3])] - backlog)
                if at <= now:
                    ready.append((prio, len(ready), name))
                else:
                    times.append(at)
            if not ready:
                now = min(times)
                continue
            name = min(ready)[2]
            prio, fn, needs, after, sends, dur, backlog = left.pop(name)
            self.log.append((now, name))
            now += dur
            for key, src, dst, to, here in sends:
                link = self.link(to)
                size = math.prod(here.shape) * jnp.dtype(here.dtype).itemsize
                free[link] = max(free[link], now) + size / self.rate[link]
                arrive[key] = free[link] + self.latency
            finished.add(name)
            out.append(name)
        self.log.append((max(now, max(free.values())), "end"))
        return out

    def link(self, to):
        return "y" if to in ("yl", "yh") else to

    def copy(self, key, src, dst, to):
        i = self.index[key]
        return pltpu.make_async_remote_copy(
            src_ref=src, dst_ref=dst, send_sem=self.ss.at[i], recv_sem=self.rs.at[i],
            device_id=self.place.dev[to], device_id_type=MESH)

    def wait(self, key):
        if key in self.done:
            return
        self.done.add(key)
        if key in self.local:
            self.local[key][0].wait()
        else:
            self.copy(key, self.recv[key], self.recv[key], "x+").wait_recv()

    def sent(self, keep):
        for key in [k for k in self.copies if keep(k)]:
            self.copies.pop(key).wait_send()

    def run(self):
        for name in self.order():
            prio, fn, needs, after, sends, dur, backlog = self.tasks[name]
            for k in needs:
                self.wait(k)
            if fn is not None:
                fn()
            for key, src, dst, to, here in sends:
                self.copies[key] = self.copy(key, src, dst, to)
                self.copies[key].start()
        for key in list(self.local) + list(self.index):
            self.wait(key)
        self.sent(lambda k: True)


WAYS = (("x+", "x-"), ("z+", "z-"))


def add_gather(plan, name, full, prio, backlogs, exchange):
    p = plan.place
    width = full.shape[1] // 2
    one, two = (p.xs, p.zs), (p.zs, p.xs)

    def view(part, yy, i, j, half=None):
        zz, xx = (j, i) if part == 0 else (i, j)
        start, n = part * width, width
        if half is not None:
            n = width // 2
            start += half * n
        return full.at[p.rows(zz, yy, xx), pl.ds(start, n)]

    own = full.at[p.rows(p.z, p.yh, p.x)]
    plan.add((name, "exchange"), exchange[0], needs=[("load", name)], after=exchange[1], backlog=exchange[2],
             sends=[((name, "y"), own, own, "yh", full.at[p.rows(p.z, 1 - p.yh, p.x)])])
    arrived = ([], [])
    for w, yy in ((0, p.yh), (1, 1 - p.yh)):
        pr = prio + w
        backlog = backlogs[w]
        start = [("load", name)] if w == 0 else [(name, "y")]
        got = arrived[w]

        def copy(key, v, to, here):
            return ((name, w) + key, v, v, to, here)

        firsts, seconds = [], []
        for q in (0, 1):
            i0, ip, im, i2 = one[q]
            j0, jp, jm, j2 = two[q]
            for s, near in ((0, im), (1, ip)):
                firsts.append(copy((q, "f", s), view(q, yy, i0, j0), WAYS[q][s], view(q, yy, near, j0)))
            for s, near in ((0, jm), (1, jp)):
                seconds.append(copy((q, 0, "s", s), view(q, yy, i0, j0), WAYS[1 - q][s], view(q, yy, i0, near)))
        plan.add((name, w, "firsts"), pr, needs=start, sends=firsts, backlog=backlog)
        plan.add((name, w, "seconds"), pr + 0.3, needs=start, sends=seconds, backlog=backlog)
        for q in (0, 1):
            i0, ip, im, i2 = one[q]
            j0, jp, jm, j2 = two[q]
            for s, i in ((0, im), (1, ip)):
                plan.add((name, w, q, "ff", s), pr, needs=[(name, w, q, "f", s)], backlog=backlog, sends=[
                    copy((q, "ff", s), view(q, yy, i, j0, s), WAYS[q][s], view(q, yy, i2, j0, s))])
            for k, i, needs in ((1, im, ["f0"]), (2, ip, ["f1"]), (3, i2, ["ff0", "ff1"])):
                plan.add((name, w, q, "s", k), pr + 0.2, needs=[(name, w, q, n[:-1], int(n[-1])) for n in needs],
                         backlog=backlog, sends=[
                    copy((q, k, "s", s), view(q, yy, i, j0), WAYS[1 - q][s], view(q, yy, i, near))
                    for s, near in ((0, jm), (1, jp))])
            for k, i in enumerate((i0, im, ip, i2)):
                for s, near in ((0, jm), (1, jp)):
                    plan.add((name, w, q, k, "sf", s), pr + 0.1, needs=[(name, w, q, k, "s", s)], backlog=backlog, sends=[
                        copy((q, k, "sf", s), view(q, yy, i, near, s), WAYS[1 - q][s], view(q, yy, i, j2, s))])
                    got += [(name, w, q, k, "s", s), (name, w, q, k, "sf", s)]
            got += [(name, w, q, "f", 0), (name, w, q, "f", 1), (name, w, q, "ff", 0), (name, w, q, "ff", 1)]
        got += start
    return arrived


def add_scatter(plan, d, far1, near1, far2, near2, keep, ys, yr, gn, prio, backlogs):
    p = plan.place
    width = d.shape[1] // 2
    one, two = (p.zs, p.xs), (p.xs, p.zs)

    def view(part, yy, i, j, half=None):
        zz, xx = (i, j) if part == 0 else (j, i)
        start, n = part * width, width
        if half is not None:
            n = width // 2
            start += half * n
        return d.at[p.rows(zz, yy, xx), pl.ds(start, n)]

    def fold(into, *terms):
        def fn():
            total = into[...].astype(f32)
            for t in terms:
                total = total + t[...].astype(f32)
            into[...] = total.astype(into.dtype)
        return fn

    for w, yy in ((0, 1 - p.yh), (1, p.yh)):
        pr = prio + w
        b = backlogs[w]
        for q in (0, 1):
            first, second = WAYS[1 - q], WAYS[q]
            j0, jp, jm, j2 = two[q]
            js = (j2, jp, jm, j0)
            slot = (3, 1, 2, 0)

            def part_of(i, k):
                return ("partial", w, i if q == 0 else slot[k])

            for k, j in enumerate(js):
                far = [("rs", w, q, "far1", k, h) for h in (0, 1)]
                near = [("rs", w, q, "near1", k, h) for h in (0, 1)]
                plan.add(("rs", w, q, "s1", k), pr + 0.1, after=[part_of(3, k)], backlog=b, sends=[
                    (far[h], view(q, yy, one[q][3], j, h), far1.at[w, q, k, h], first[h], far1.at[w, q, k, h])
                    for h in (0, 1)])
                for h in (0, 1):
                    i = 1 + h
                    plan.add(("rs", w, q, "s2", k, h), pr + 0.05 * k / 4, fold(view(q, yy, one[q][i], j, h), far1.at[w, q, k, h]),
                             needs=[far[h]], after=[part_of(i, k)], dur=0.15, backlog=b, sends=[
                        (near[h], view(q, yy, one[q][i], j), near1.at[w, q, k, h], first[h], near1.at[w, q, k, h])])
                mine = view(q, yy, one[q][0], j)
                if k < 3:
                    fn = fold(mine, near1.at[w, q, k, 0], near1.at[w, q, k, 1])
                else:
                    def fn(mine=mine, w=w, q=q, k=k):
                        keep[w, q] = (mine[...].astype(f32) + near1[w, q, k, 0].astype(f32)
                                      + near1[w, q, k, 1].astype(f32))
                plan.add(("rs", w, q, "s3", k), pr - 0.1, fn, needs=near, after=[part_of(0, k)], dur=0.25, sends=[
                    (("rs", w, q, "far2", h), view(q, yy, one[q][0], j, h), far2.at[w, q, h], second[h], far2.at[w, q, h])
                    for h in (0, 1)] if k == 0 else [])
            for h in (0, 1):
                plan.add(("rs", w, q, "t2", h), pr - 0.2, fold(view(q, yy, one[q][0], two[q][1 + h], h), far2.at[w, q, h]),
                         needs=[("rs", w, q, "far2", h)], after=[("rs", w, q, "s3", 1 + h)], dur=0.15, sends=[
                    (("rs", w, q, "near2", h), view(q, yy, one[q][0], two[q][1 + h]), near2.at[w, q, h], second[h],
                     near2.at[w, q, h])])
            cols = pl.ds(q * width, width)

            def total(w=w, q=q):
                return keep[w, q] + near2[w, q, 0].astype(f32) + near2[w, q, 1].astype(f32)

            needs = [("rs", w, q, "near2", h) for h in (0, 1)]
            if w == 0:
                def fn(total=total, cols=cols):
                    ys[:, cols] = total()
                plan.add(("rs", "yh", q), pr - 0.3, fn, needs=needs, after=[("rs", w, q, "s3", 3)], dur=0.2,
                         sends=[(("yh", q), ys.at[:, cols], yr.at[:, cols], "yh", yr.at[:, cols])])
            else:
                def fn(total=total, cols=cols):
                    gn[:, cols] = (total() + yr[:, cols]).astype(bf16)
                plan.add(("rs", "end", q), pr - 0.3, fn, needs=needs + [("yh", q)], after=[("rs", w, q, "s3", 3)], dur=0.2)


def kernel(scale, n_in, c_in, h_in, g_in, wi_in, wo_in, wp_in,
           gn_out, gc_out, gwi_out, gwo_out, gwp_out,
           G, N, ACT, CTX, HP, WIN, WOUT, WPROJ, GH, SLOPE, P1S, P1R, POWN, P2S, P2R,
           C1S, C1R, COWN, C2S, C2R, FAR1, NEAR1, FAR2, NEAR2, KEEP, YS, YR, ss, rs, ls):
    block = g_in.shape[0]
    p = Place(block)
    z, yh, x, gz, yl, c = p.z, p.yh, p.x, p.gz, p.yl, p.c
    o = 1 - yh
    n = 4 * block
    plan = Plan(p, ss, rs)
    other_y, other_c, other_yc = (1 - yl) * 2 + c, yl * 2 + 1 - c, (1 - yl) * 2 + 1 - c

    bar = pltpu.get_barrier_semaphore()
    for d in p.dev.values():
        pl.semaphore_signal(bar, inc=1, device_id=d, device_id_type=MESH)
    for i, (name, src, dst, at) in enumerate((
            ("g", g_in, G.at[p.rows(z, yh, x)], 0.0), ("h", h_in, HP, 0.0), ("c", c_in, CTX.at[gz], 0.0),
            ("n", n_in, N.at[p.rows(z, yh, x)], 0.0), ("wo", wo_in, WOUT, 1.0), ("wp", wp_in, WPROJ, 2.0),
            ("wi", wi_in, WIN, 3.0))):
        plan.load(("load", name), pltpu.make_async_copy(src, dst, ls.at[i]), at)
    pl.semaphore_wait(bar, len(p.dev))

    g_got = add_gather(plan, "g", G, 0, K["g"], (-1, (), 0.5))
    n_got = add_gather(plan, "n", N, 20, K["n"], K["nx"])

    def spread(key, view, prio, needs=(), after=(), fn=None, dur=0.1, backlog=1e9, relay=None):
        plan.add(key + ("spread",), prio, fn, needs=needs, after=after, dur=dur, backlog=backlog, sends=[
            (key + ("y",), view(gz), view(gz), "yl", view(other_y)),
            (key + ("c",), view(gz), view(gz), "c", view(other_c))])
        plan.add(key + ("relay",), prio + 0.1 if relay is None else relay, needs=[key + ("y",)], sends=[
            (key + ("cy",), view(other_y), view(other_y), "c", view(other_yc))])
        return [key + (k,) for k in ("y", "c", "cy")]

    act_got = []
    pieces = K["pieces"]
    half_rows = HP.shape[0] // pieces
    for half in range(pieces):
        def gelu(half=half):
            @pl.loop(0, half_rows // 16)
            def _(i):
                here = pl.ds(pl.multiple_of(half * half_rows + i * 16, 16), 16)
                v = HP[here, :].astype(f32)
                cdf = 0.5 * (1.0 + lax.erf(v * inv_root_two))
                density = jnp.exp(-0.5 * v * v) * inv_root_two_pi
                SLOPE[here, :] = cdf + v * density
                there = pl.ds(pl.multiple_of((gz * pieces + half) * half_rows + i * 16, 16), 16)
                ACT[there, :] = (v * cdf).astype(bf16)

        plan.add(("gelu", half), 1.5, gelu, needs=[("load", "h")], after=[("g", 0, "seconds")], dur=1.2 / pieces)
        act_got += spread(("act", half), lambda j, half=half: ACT.at[pl.ds(
            pl.multiple_of((j * pieces + half) * half_rows, half_rows), half_rows)], K["act"], after=[("gelu", half), ("g", "exchange")],
            backlog=K["ab"])
    ctx_got = spread(("ctx",), lambda j: CTX.at[j], K["ctx"], needs=[("load", "c")], after=[("g", "exchange")],
                     backlog=K["ab"])

    wave_yh = (yh, o)
    gh_got = ([], [])
    sub = n // 2
    for w in (0, 1):
        for s, yy in enumerate((1 - yl, yl)):
            def peer(w=w, s=s, yy=yy):
                P1S[w, s] = nt(G[p.chunk(yy * 2 + 1 - c, wave_yh[w]), :], WOUT[...])

            def own(w=w, s=s, yy=yy):
                v = nt(G[p.chunk(yy * 2 + c, wave_yh[w]), :], WOUT[...]) + P1R[w, s]
                if s == 0:
                    P2S[w] = v.astype(bf16)
                else:
                    POWN[w] = v

            plan.add(("p1", w, s), 3 + 0.1 * s, peer, needs=g_got[w] + [("load", "wo")], dur=0.95,
                     after=[("p1", w, 0)] if s else [], sends=[
                (("p1", w, s), P1S.at[w, s], P1R.at[w, s], "c", P1R.at[w, s])])
            plan.add(("own", w, s), 3.2 + 0.1 * s, own, needs=[("p1", w, s)], after=[("p1", w, 1)], dur=1.0, sends=[
                (("p2", w, h), P2S.at[w, pl.ds(h * sub, sub)], P2R.at[w, pl.ds(h * sub, sub)], "yl",
                 P2R.at[w, pl.ds(h * sub, sub)]) for h in (0, 1)] if s == 0 else [])
        for h in (0, 1):
            def hidden(w=w, h=h):
                here = pl.ds(h * sub, sub)
                local = pl.ds(pl.multiple_of(wave_yh[w] * n + h * sub, sub), sub)
                rows = pl.ds(pl.multiple_of((gz * 2 + wave_yh[w]) * n + h * sub, sub), sub)
                GH[rows, :] = ((POWN[w, here] + P2R[w, here].astype(f32)) * SLOPE[local, :]).astype(bf16)

            gh_got[w].extend(spread(("gh", w, h), lambda j, w=w, h=h: GH.at[pl.ds(
                pl.multiple_of((j * 2 + wave_yh[w]) * n + h * sub, sub), sub)], 2, fn=hidden, needs=[("p2", w, h)],
                after=[("own", w, 1)] + [("gelu", i) for i in range(pieces)], dur=0.3))

    g_all = g_got[0] + g_got[1]
    for s, yy in enumerate((1 - yl, yl)):
        def peer(s=s, yy=yy):
            C1S[s] = nt(WPROJ[...], G[p.shard(yy * 2 + 1 - c), :])

        def own(s=s, yy=yy):
            v = nt(WPROJ[...], G[p.shard(yy * 2 + c), :]) + C1R[s]
            if s == 0:
                C2S[...] = v.astype(bf16)
            else:
                COWN[...] = v

        plan.add(("c1", s), 30 + s, peer, needs=g_all + [("load", "wp")], dur=0.6,
                 after=[("c1", 0)] if s else [], sends=[
            (("c1", s), C1S.at[s], C1R.at[s], "c", C1R.at[s])])
        plan.add(("cown", s), 32 + s, own, needs=[("c1", s)], after=[("c1", 1)], dur=0.6)

    plan.add(("c2",), 60, needs=[], after=[("cown", 0), ("gh", 1, 0, "spread"), ("gh", 1, 1, "spread")],
             sends=[(("c2",), C2S, C2R, "yl", C2R)])

    def ctx_done():
        gc_out[...] = (COWN[...] + C2R[...].astype(f32)).astype(bf16)

    plan.add(("gc",), 70, ctx_done, needs=[("c2",)], after=[("cown", 1)], dur=0.1)

    readers = [("own", w, s) for w in (0, 1) for s in (0, 1)] + [("cown", 0), ("cown", 1)]
    for f in range(WOUT.shape[0] // 256):
        for t in range(3):
            def tile(f=f, t=t):
                rows, cols = pl.ds(f * 256, 256), pl.ds(t * 512, 512)
                gwo_out[rows, cols] = (tn(ACT[:, rows], G[:, cols]) * scale).astype(bf16)

            plan.add(("wo", f, t), 40, tile, needs=g_all + act_got, dur=0.75)
            readers.append(("wo", f, t))
    for t in range(3):
        def tile(t=t):
            cols = pl.ds(t * 512, 512)
            total = nn(CTX[0], G[p.shard(0), cols])
            for j in range(1, 4):
                total += nn(CTX[j], G[p.shard(j), cols])
            gwp_out[:, cols] = (total * scale).astype(bf16)

        plan.add(("wp", t), 46, tile, needs=g_all + ctx_got, dur=0.65)
    readers += [("wp", t) for t in range(3)]

    plan.add(("g", "sent"), 48, lambda: plan.sent(lambda k: k[0] == "g"), after=readers
             + [k for k in plan.tasks if k[0] == "g"], dur=0.1)
    for w, yy in ((0, o), (1, yh)):
        for i in (3, 1, 2, 0):
            def partial(i=i, yy=yy):
                rows = p.chunk(p.zs[i], yy)
                G[rows, :] = nt(GH[rows, :], WIN[...]).astype(bf16)

            plan.add(("partial", w, i), 4 + w * 8 + 0.01 * ((3, 1, 2, 0).index(i)), partial, needs=gh_got[1 - w] + [("load", "wi")],
                     after=[("g", "sent"), ("gh", 1 - w, 0, "spread"), ("gh", 1 - w, 1, "spread")], dur=1.0)
    add_scatter(plan, G, FAR1, NEAR1, FAR2, NEAR2, KEEP, YS, YR, gn_out, 7, K["rs"])

    parts = [("partial", w, i) for w in (0, 1) for i in range(4)]
    for t in range(N.shape[1] // 256):
        def tile(t=t):
            cols = pl.ds(t * 256, 256)
            gwi_out[cols, :] = (tn(N[:, cols], GH[...]) * scale).astype(bf16)

        plan.add(("wi", t), 80, tile, needs=n_got[0] + n_got[1], after=parts, dur=1.1)

    plan.run()


def copy_out(*refs):
    copies = [pltpu.make_async_copy(refs[i], refs[5 + i], refs[10].at[i]) for i in range(5)]
    for c in copies:
        c.start()
    for c in copies:
        c.wait()


def body(normed, context, hidden_pre, grad_out, w_in, w_out, w_proj):
    block, width = grad_out.shape
    shard, hidden = hidden_pre.shape
    feats = context.shape[1]
    tokens = 32 * block
    chunk = 4 * block
    half = width // 2
    scratch = [
        pltpu.VMEM((tokens, width), bf16),
        pltpu.VMEM((tokens, width), bf16),
        pltpu.VMEM((tokens, hidden), bf16),
        pltpu.VMEM((4, feats, shard), bf16),
        pltpu.VMEM((shard, hidden), bf16),
        pltpu.VMEM(w_in.shape, bf16),
        pltpu.VMEM(w_out.shape, bf16),
        pltpu.VMEM(w_proj.shape, bf16),
        pltpu.VMEM((tokens, hidden), bf16),
        pltpu.VMEM((shard, hidden), f32),
        pltpu.VMEM((2, 2, chunk, hidden), f32),
        pltpu.VMEM((2, 2, chunk, hidden), f32),
        pltpu.VMEM((2, chunk, hidden), f32),
        pltpu.VMEM((2, chunk, hidden), bf16),
        pltpu.VMEM((2, chunk, hidden), bf16),
        pltpu.VMEM((2, feats, shard), f32),
        pltpu.VMEM((2, feats, shard), f32),
        pltpu.VMEM((feats, shard), f32),
        pltpu.VMEM((feats, shard), bf16),
        pltpu.VMEM((feats, shard), bf16),
        pltpu.VMEM((2, 2, 4, 2, block, half // 2), bf16),
        pltpu.VMEM((2, 2, 4, 2, block, half), bf16),
        pltpu.VMEM((2, 2, 2, block, half // 2), bf16),
        pltpu.VMEM((2, 2, 2, block, half), bf16),
        pltpu.VMEM((2, 2, block, half), f32),
        pltpu.VMEM((block, width), f32),
        pltpu.VMEM((block, width), f32),
        pltpu.SemaphoreType.DMA((SEMS,)),
        pltpu.SemaphoreType.DMA((SEMS,)),
        pltpu.SemaphoreType.DMA((8,)),
    ]
    context = context.T
    outs = [normed, context, w_in, w_out, w_proj]

    def call(*refs):
        kernel(1.0 / math.sqrt(tokens), *refs)

    results = pl.pallas_call(
        call,
        out_shape=[pltpu.VMEM(v.shape, v.dtype) for v in outs],
        in_specs=[pl.BlockSpec(memory_space=pl.ANY)] * 7,
        out_specs=[pl.BlockSpec(memory_space=pltpu.VMEM)] * 5,
        scratch_shapes=scratch,
        compiler_params=pltpu.CompilerParams(
            collective_id=0, has_side_effects=True, vmem_limit_bytes=56 * 2**20),
    )(normed, context, hidden_pre, grad_out, w_in, w_out, w_proj)
    gn, gc, gwi, gwo, gwp = pl.pallas_call(
        copy_out,
        out_shape=[jax.ShapeDtypeStruct(v.shape, v.dtype) for v in outs],
        in_specs=[pl.BlockSpec(memory_space=pltpu.VMEM)] * 5,
        out_specs=[pl.BlockSpec(memory_space=pl.ANY)] * 5,
        scratch_shapes=[pltpu.SemaphoreType.DMA((5,))],
        compiler_params=pltpu.CompilerParams(vmem_limit_bytes=2**20),
    )(*results)
    return gn, gc.T, gwi, gwo, gwp


def solution(mesh):
    in_specs = (
        P(("gx", "gy"), "gz"),
        P("gz", ("gx", "gy")),
        P("gz", ("gx", "gy")),
        P(("gx", "gy"), "gz"),
        P("gz", ("gx", "gy")),
        P(("gx", "gy"), "gz"),
        P(("gx", "gy"), "gz"),
    )
    out_specs = (
        P(("gx", "gy"), "gz"),
        P("gz", ("gx", "gy")),
        P("gz", ("gx", "gy")),
        P(("gx", "gy"), "gz"),
        P(("gx", "gy"), "gz"),
    )
    return jax.shard_map(body, mesh=mesh, in_specs=in_specs, out_specs=out_specs, check_vma=False)
```

time: 713 us -> 147 us (0.21)
  waiting for transfers between devices: 612 us -> 0 us
  Pallas kernels: 0 us -> 145 us
  matrix products: 58.3 us -> 0 us
  blocking collectives: 15.5 us -> 0 us
  between operations: 14.1 us -> 0.82 us
    reduce_scatter x3 -> x0, waiting for transfers between devices: 345 us -> none  [the longest x1 252 us: body(): lax.psum_scatter(contract_cols(panel, w_in), ('gx', 'gy'), scatter_dimens...]
    all_gather x4 -> x0, waiting for transfers between devices: 265 us -> none  [the longest x1 107 us: body(): lax.all_gather(grad_out, ('gx', 'gy'), axis=0, tiled=True)]
    pallas_call x0 -> x2, Pallas kernels: none -> 145 us  [the longest x1 143 us: body(): pl.pallas_call(call, out_shape=[pltpu.VMEM(v.shape, v.dtype) for v in out...]
    dot_general x6 -> x0, matrix products: 58.3 us -> none  [the longest x3 29.9 us: contract_cols(): lax.dot_general(left, right, (((1,), (1,)), ((), ())), preferred_element_...]
    all_gather x1 -> x0, blocking collectives: 15.5 us -> none  [body(): lax.all_gather(context, 'gz', axis=0, tiled=True)]
  transfers between devices with their start and end apart: 7 -> 0, of which waited for: 7 -> 0; matrix products, arithmetic and copies ran while one was open for 7% -> 0% of each run, Pallas kernels for 0% -> 0%
where the time goes in v3:
time: 147 us; the launch traced here: 146 us
  Pallas kernels  145 us (99%)
    pallas_call x1, Pallas kernels, body(): pl.pallas_call(call, out_shape=[pltpu.VMEM(v.shape, v.dtype) for v in out...  143 us

profile of v3, /device:TPU:0, one launch (start us, length us, event | category | flops | bytes accessed | tf_op | source)
XLA Modules:
  0.0 146.3 jit_solution(15289147464012970106)
XLA Ops:
  0.6 142.9 %shard_map.110 = (bf16[80,1536]{1,0:T(8,128)(2,1)S(1)}, bf16[192,640]{1,0:T(8,128)(2,1)S(1)}, bf16[1536,768]{1,0:T(8,128)(2,1)S(1)}, bf16[768,1536]{1,0:T(8,128)(2,1)S(1)}, bf16[192,1536]{1,0:T(8,128)(2,1)S(1)}) custom-call(bf16[80,1536]{1,0:T(8,128)(2,1)} %refs_0_.1, bf16[192,640]{1,0:T(8,128)(2,1)} %bitcast.2, bf16[640,768]{1,0:T(8,128)(2,1)} %refs_2_.1, ...), custom_call_target="tpu_custom_call" | custom-call | tf_op jit(solution)/shard_map/pallas_call | solution.py:497
  143.5 2.6 %shard_map.111 = (bf16[80,1536]{1,0:T(8,128)(2,1)}, bf16[192,640]{1,0:T(8,128)(2,1)}, bf16[1536,768]{1,0:T(8,128)(2,1)}, bf16[768,1536]{1,0:T(8,128)(2,1)}, bf16[192,1536]{1,0:T(8,128)(2,1)}) custom-call(bf16[80,1536]{1,0:T(8,128)(2,1)S(1)} %get-tuple-element.15.refs_0_, bf16[192,640]{1,0:T(8,128)(2,1)S(1)} %get-tuple-element.16.refs_1_, ...), custom_call_target="tpu_custom_call" | custom-call | tf_op jit(solution)/shard_map/pallas_call | solution.py:506

commit v4 on v3

--- a/solution.py
+++ b/solution.py
@@ -13,6 +13,81 @@
 inv_root_two_pi = 0.3989422804014327
 SEMS = 352
 K = dict(g=(1e9, 2.5), n=(2.5, 2.5), nx=(1, (("gh", 0, 1, "spread"),), 1e9), act=12, ctx=13, rs=(1e9, 1.0), ab=0.5, pieces=4)
+
+TUNE = {
+    ('act', 'relay'): (-36.05, None),
+    ('act', 'spread'): (2.79, 1.0),
+    ('c1',): (-4.12, 1.5),
+    ('c2',): (25.01, 0.5),
+    ('cown',): (-9.27, 0.5),
+    ('ctx', 'relay'): (-22.54, 0.5),
+    ('ctx', 'spread'): (55.46, 1.5),
+    ('g', 'exchange'): (9.02, 4.0),
+    ('g', 'sent'): (-19.85, 0.5),
+    ('g', 0, 'ff'): (-29.46, 4.0),
+    ('g', 0, 'firsts'): (8.89, 3.0),
+    ('g', 0, 's'): (-27.07, 2.5),
+    ('g', 0, 'seconds'): (-3.13, 2.5),
+    ('g', 0, 'sf'): (7.86, None),
+    ('g', 1, 'ff'): (7.52, 6.0),
+    ('g', 1, 'firsts'): (13.91, None),
+    ('g', 1, 's'): (12.11, 1.0),
+    ('g', 1, 'seconds'): (5.76, 2.5),
+    ('g', 1, 'sf'): (-40.36, 1e9),
+    ('gc',): (-24.56, None),
+    ('gelu',): (-13.85, 2.5),
+    ('gh', 0, 'relay'): (30.97, 3.0),
+    ('gh', 0, 'spread'): (-14.58, 3.0),
+    ('gh', 1, 'relay'): (-20.72, None),
+    ('gh', 1, 'spread'): (17.11, 4.0),
+    ('n', 'exchange'): (26.73, 4.0),
+    ('n', 0, 'ff'): (16.27, 4.0),
+    ('n', 0, 'firsts'): (-3.65, 1.0),
+    ('n', 0, 's'): (-21.35, 0.5),
+    ('n', 0, 'seconds'): (1.58, 3.0),
+    ('n', 0, 'sf'): (15.74, None),
+    ('n', 1, 'ff'): (-58.75, 2.0),
+    ('n', 1, 'firsts'): (-1.73, 1.0),
+    ('n', 1, 's'): (-16.0, 3.0),
+    ('n', 1, 'seconds'): (0.81, 6.0),
+    ('n', 1, 'sf'): (-18.02, None),
+    ('own', 0): (-4.16, 1.5),
+    ('own', 1): (33.36, 2.5),
+    ('p1', 0): (-37.69, 4.0),
+    ('p1', 1): (-22.43, None),
+    ('partial', 0): (45.97, 6.0),
+    ('partial', 1): (-1.22, 2.0),
+    ('rs', 'end'): (39.5, 2.0),
+    ('rs', 'yh'): (-20.47, 2.5),
+    ('rs', 0, 's1'): (-22.5, None),
+    ('rs', 0, 's2'): (-37.73, None),
+    ('rs', 0, 's3'): (17.91, 6.0),
+    ('rs', 0, 't2'): (-5.6, 2.5),
+    ('rs', 1, 's1'): (-6.41, 4.0),
+    ('rs', 1, 's2'): (-3.32, 0.5),
+    ('rs', 1, 's3'): (-1.37, None),
+    ('rs', 1, 't2'): (32.44, None),
+    ('wi',): (25.65, 2.0),
+    ('wo',): (1.57, 1.5),
+    ('wp',): (38.35, 1.0),
+}
+LATENCY, STRETCH, PER_COPY = 2.235, 1.417, 0.03
+
+
+def group(n):
+    if n[0] in ("g", "n"):
+        if len(n) <= 3:
+            return n
+        return (n[0], n[1], n[3] if n[3] in ("ff", "s") else n[4])
+    if n[0] == "rs":
+        return n[:2] if n[1] in ("yh", "end") else ("rs", n[1], n[3])
+    if n[0] == "gh":
+        return ("gh", n[1], n[3])
+    if n[0] == "act":
+        return ("act", n[2])
+    if n[0] in ("partial", "p1", "own"):
+        return n[:2]
+    return n[:1] if n[0] in ("wo", "wp", "wi", "c1", "cown", "gelu") else n
 
 
 def nt(left, right):
@@ -62,7 +137,7 @@
 
 class Plan:
     rate = {"x+": 46e3, "x-": 46e3, "z+": 46e3, "z-": 46e3, "y": 46e3, "c": 6e5}
-    latency = 1.5
+    latency = LATENCY
 
     def __init__(self, place, send_sems, recv_sems):
         self.place, self.ss, self.rs = place, send_sems, recv_sems
@@ -74,6 +149,8 @@
         self.local[key] = (copy, at)
 
     def add(self, name, prio, fn=None, needs=(), after=(), sends=(), dur=0.1, backlog=1e9):
+        shift, queue = TUNE.get(group(name), (0.0, None))
+        prio, backlog = prio + shift, backlog if queue is None else queue
         self.tasks[name] = (prio, fn, tuple(needs), tuple(after), tuple(sends), dur, backlog)
         for key, src, dst, to, here in sends:
             self.index[key] = len(self.index)
@@ -102,11 +179,11 @@
             name = min(ready)[2]
             prio, fn, needs, after, sends, dur, backlog = left.pop(name)
             self.log.append((now, name))
-            now += dur
+            now += dur * STRETCH
             for key, src, dst, to, here in sends:
                 link = self.link(to)
                 size = math.prod(here.shape) * jnp.dtype(here.dtype).itemsize
-                free[link] = max(free[link], now) + size / self.rate[link]
+                free[link] = max(free[link], now) + size / self.rate[link] + PER_COPY
                 arrive[key] = free[link] + self.latency
             finished.add(name)
             out.append(name)

time: 147 us -> 140 us (0.952)
  Pallas kernels: 145 us -> 139 us
    pallas_call x1, Pallas kernels: 143 us -> 136 us  [body(): pl.pallas_call(call, out_shape=[pltpu.VMEM(v.shape, v.dtype) for v in out...]
where the time goes in v4:
time: 140 us
  Pallas kernels  139 us (99%)
    pallas_call x1, Pallas kernels, body(): pl.pallas_call(call, out_shape=[pltpu.VMEM(v.shape, v.dtype) for v in out...  136 us

profile of v4, /device:TPU:0, one launch (start us, length us, event | category | flops | bytes accessed | tf_op | source)
XLA Modules:
  0.0 139.8 jit_solution(16464959455638481360)
XLA Ops:
  0.6 136.4 %shard_map.110 = (bf16[80,1536]{1,0:T(8,128)(2,1)S(1)}, bf16[192,640]{1,0:T(8,128)(2,1)S(1)}, bf16[1536,768]{1,0:T(8,128)(2,1)S(1)}, bf16[768,1536]{1,0:T(8,128)(2,1)S(1)}, bf16[192,1536]{1,0:T(8,128)(2,1)S(1)}) custom-call(bf16[80,1536]{1,0:T(8,128)(2,1)} %refs_0_.1, bf16[192,640]{1,0:T(8,128)(2,1)} %bitcast.2, bf16[640,768]{1,0:T(8,128)(2,1)} %refs_2_.1, ...), custom_call_target="tpu_custom_call" | custom-call | tf_op jit(solution)/shard_map/pallas_call | solution.py:574
  137.1 2.6 %shard_map.111 = (bf16[80,1536]{1,0:T(8,128)(2,1)}, bf16[192,640]{1,0:T(8,128)(2,1)}, bf16[1536,768]{1,0:T(8,128)(2,1)}, bf16[768,1536]{1,0:T(8,128)(2,1)}, bf16[192,1536]{1,0:T(8,128)(2,1)}) custom-call(bf16[80,1536]{1,0:T(8,128)(2,1)S(1)} %get-tuple-element.15.refs_0_, bf16[192,640]{1,0:T(8,128)(2,1)S(1)} %get-tuple-element.16.refs_1_, ...), custom_call_target="tpu_custom_call" | custom-call | tf_op jit(solution)/shard_map/pallas_call | solution.py:583

commit v5 on v4

--- a/solution.py
+++ b/solution.py
@@ -383,6 +383,17 @@
             ("n", n_in, N.at[p.rows(z, yh, x)], 0.0), ("wo", wo_in, WOUT, 1.0), ("wp", wp_in, WPROJ, 2.0),
             ("wi", wi_in, WIN, 3.0))):
         plan.load(("load", name), pltpu.make_async_copy(src, dst, ls.at[i]), at)
+    plan.wait(("load", "h"))
+
+    @pl.loop(0, HP.shape[0] // 16)
+    def _(i):
+        here = pl.ds(pl.multiple_of(i * 16, 16), 16)
+        v = HP[here, :].astype(f32)
+        cdf = 0.5 * (1.0 + lax.erf(v * inv_root_two))
+        density = jnp.exp(-0.5 * v * v) * inv_root_two_pi
+        SLOPE[here, :] = cdf + v * density
+        ACT[pl.ds(pl.multiple_of(gz * HP.shape[0] + i * 16, 16), 16), :] = (v * cdf).astype(bf16)
+
     pl.semaphore_wait(bar, len(p.dev))
 
     g_got = add_gather(plan, "g", G, 0, K["g"], (-1, (), 0.5))
@@ -400,18 +411,7 @@
     pieces = K["pieces"]
     half_rows = HP.shape[0] // pieces
     for half in range(pieces):
-        def gelu(half=half):
-            @pl.loop(0, half_rows // 16)
-            def _(i):
-                here = pl.ds(pl.multiple_of(half * half_rows + i * 16, 16), 16)
-                v = HP[here, :].astype(f32)
-                cdf = 0.5 * (1.0 + lax.erf(v * inv_root_two))
-                density = jnp.exp(-0.5 * v * v) * inv_root_two_pi
-                SLOPE[here, :] = cdf + v * density
-                there = pl.ds(pl.multiple_of((gz * pieces + half) * half_rows + i * 16, 16), 16)
-                ACT[there, :] = (v * cdf).astype(bf16)
-
-        plan.add(("gelu", half), 1.5, gelu, needs=[("load", "h")], after=[("g", 0, "seconds")], dur=1.2 / pieces)
+        plan.add(("gelu", half), 1.5, needs=[("load", "h")], after=[("g", 0, "seconds")], dur=1.2 / pieces)
         act_got += spread(("act", half), lambda j, half=half: ACT.at[pl.ds(
             pl.multiple_of((j * pieces + half) * half_rows, half_rows), half_rows)], K["act"], after=[("gelu", half), ("g", "exchange")],
             backlog=K["ab"])

time: 140 us -> 142 us (1.014)
  no operation moved by 1% of the time
where the time goes in v5:
time: 142 us; the launch traced here: 141 us
  Pallas kernels  140 us (99%)
    pallas_call x1, Pallas kernels, body(): pl.pallas_call(call, out_shape=[pltpu.VMEM(v.shape, v.dtype) for v in out...  138 us

profile of v5, /device:TPU:0, one launch (start us, length us, event | category | flops | bytes accessed | tf_op | source)
XLA Modules:
  0.0 141.1 jit_solution(369580024482113302)
XLA Ops:
  0.6 137.7 %shard_map.110 = (bf16[80,1536]{1,0:T(8,128)(2,1)S(1)}, bf16[192,640]{1,0:T(8,128)(2,1)S(1)}, bf16[1536,768]{1,0:T(8,128)(2,1)S(1)}, bf16[768,1536]{1,0:T(8,128)(2,1)S(1)}, bf16[192,1536]{1,0:T(8,128)(2,1)S(1)}) custom-call(bf16[80,1536]{1,0:T(8,128)(2,1)} %refs_0_.1, bf16[192,640]{1,0:T(8,128)(2,1)} %bitcast.2, bf16[640,768]{1,0:T(8,128)(2,1)} %refs_2_.1, ...), custom_call_target="tpu_custom_call" | custom-call | tf_op jit(solution)/shard_map/pallas_call | solution.py:574
  138.4 2.6 %shard_map.111 = (bf16[80,1536]{1,0:T(8,128)(2,1)}, bf16[192,640]{1,0:T(8,128)(2,1)}, bf16[1536,768]{1,0:T(8,128)(2,1)}, bf16[768,1536]{1,0:T(8,128)(2,1)}, bf16[192,1536]{1,0:T(8,128)(2,1)}) custom-call(bf16[80,1536]{1,0:T(8,128)(2,1)S(1)} %get-tuple-element.15.refs_0_, bf16[192,640]{1,0:T(8,128)(2,1)S(1)} %get-tuple-element.16.refs_1_, ...), custom_call_target="tpu_custom_call" | custom-call | tf_op jit(solution)/shard_map/pallas_call | solution.py:583
